TPU v7x, 32 devices: a whole 2x2x4 slice. The times are simulated.
32 devices in a mesh: dp: 8 (over y, x, core), head: 4 (over z).
Axes of the slice: x: 2, y: 2, z: 4, core: 2. Of those that a mesh axis runs over, the one named last changes fastest.
Arguments:
- tokens: bfloat16 [24, 2048, 768], P('dp', 'head'), may hold values from -6 to 6
- lengths: int32 [24], P('dp'), may hold values from 128 to 2048, as said below
- weight_in: float32 [768, 2304], P(('dp', 'head')), may hold values from -0.21875 to 0.21875
- bias_in: float32 [2304], P(('dp', 'head')), may hold values from -3 to 3
- weight_out: float32 [768, 768], P(('dp', 'head')), may hold values from -6 to 6
- bias_out: float32 [768], P(('dp', 'head')), may hold values from -2 to 2
- gain_one: float32 [768], P(('dp', 'head')), may hold values from 0.25 to 1.75
- shift_one: float32 [768], P(('dp', 'head')), may hold values from -2 to 2
- weight_up: float32 [768, 3072], P(('dp', 'head')), may hold values from -0.21875 to 0.21875
- bias_up: float32 [3072], P(('dp', 'head')), may hold values from -2 to 2
- weight_down: float32 [3072, 768], P(('dp', 'head')), may hold values from -0.109375 to 0.109375
- bias_down: float32 [768], P(('dp', 'head')), may hold values from -2 to 2
- gain_two: float32 [768], P(('dp', 'head')), may hold values from 0.25 to 1.75
- shift_two: float32 [768], P(('dp', 'head')), may hold values from -2 to 2
- cotangent: bfloat16 [24, 2048, 768], P('dp', 'head'), may hold values from -6 to 6
Outputs:
- activations: bfloat16 [24, 2048, 768], P('dp', 'head')
- input_grad: float32 [24, 2048, 768], P('dp', 'head')
- grad_weight_in: float32 [768, 2304], P(('dp', 'head'))
- grad_bias_in: float32 [1536], P(('dp', 'head'))
- grad_bias_value: float32 [768], P(('dp', 'head'))
- grad_weight_out: float32 [768, 768], P(('dp', 'head'))
- grad_bias_out: float32 [768], P(('dp', 'head'))
- grad_gain_one: float32 [768], P(('dp', 'head'))
- grad_shift_one: float32 [768], P(('dp', 'head'))
- grad_weight_up: float32 [768, 3072], P(('dp', 'head'))
- grad_bias_up: float32 [3072], P(('dp', 'head'))
- grad_weight_down: float32 [3072, 768], P(('dp', 'head'))
- grad_bias_down: float32 [768], P(('dp', 'head'))
- grad_gain_two: float32 [768], P(('dp', 'head'))
- grad_shift_two: float32 [768], P(('dp', 'head'))
Inputs may be any that keep to these rules, and one draw needn't show every extreme that they name: `lengths`: in each aligned group of 3 sequences, one, chosen by the seed, has length 2048.
All inputs are finite; a program needn't handle non-finite values.
Results may differ from a plain program's by a relative error of at most 0.015.
Values may be sent and summed in bfloat16 or wider, within the bound.
A program may use at most 384 MiB of HBM per device.

v0:
```python
from functools import partial
import math

import jax
import jax.numpy as jnp
from jax import lax
from jax.sharding import PartitionSpec as P

HD = 64
BLOCK = 64


def attend(query_cos, query_sin, key_cos, key_sin, values, block):
    batch, length, heads, width = query_cos.shape
    count = length // block
    highest = lax.Precision.HIGHEST

    def blocks(array):
        return array.reshape(batch, count, block, heads, width)

    query_cos, query_sin, key_cos, key_sin, values = (
        blocks(query_cos),
        blocks(query_sin),
        blocks(key_cos),
        blocks(key_sin),
        blocks(values),
    )
    scores = jnp.einsum("bnihe,bnjhe->bnhij", query_cos, key_cos, precision=highest)
    scores = scores + jnp.einsum("bnihe,bnjhe->bnhij", query_sin, key_sin, precision=highest)
    lower = jnp.tril(jnp.ones((block, block), jnp.float32))
    scores = scores * lower
    inner_num = jnp.einsum("bnhij,bnjhe->bnihe", scores, values, precision=highest)
    inner_den = jnp.transpose(jnp.sum(scores, axis=-1), (0, 1, 3, 2))
    state_cos = jnp.einsum("bnjhe,bnjhf->bnhef", key_cos, values, precision=highest)
    state_sin = jnp.einsum("bnjhe,bnjhf->bnhef", key_sin, values, precision=highest)
    total_cos = jnp.sum(key_cos, axis=2)
    total_sin = jnp.sum(key_sin, axis=2)
    prior_cos = jnp.cumsum(state_cos, axis=1) - state_cos
    prior_sin = jnp.cumsum(state_sin, axis=1) - state_sin
    before_cos = jnp.cumsum(total_cos, axis=1) - total_cos
    before_sin = jnp.cumsum(total_sin, axis=1) - total_sin
    outer_num = jnp.einsum("bnihe,bnhef->bnihf", query_cos, prior_cos, precision=highest)
    outer_num = outer_num + jnp.einsum(
        "bnihe,bnhef->bnihf", query_sin, prior_sin, precision=highest
    )
    outer_den = jnp.einsum("bnihe,bnhe->bnih", query_cos, before_cos, precision=highest)
    outer_den = outer_den + jnp.einsum("bnihe,bnhe->bnih", query_sin, before_sin, precision=highest)
    numer = inner_num + outer_num
    denom = inner_den + outer_den
    result = numer / jnp.maximum(denom, 1.0)[..., None]
    return result.reshape(batch, length, heads, width)


def norm(value, gain, shift):
    centered = value - jnp.mean(value, axis=-1, keepdims=True)
    spread = jnp.mean(centered * centered, axis=-1, keepdims=True)
    return centered * lax.rsqrt(spread + 1e-05) * gain + shift


def features(mixed, valid, cosine, sine):
    width = mixed.shape[1] // 3
    query_feat = jax.nn.softplus(mixed[:, :width]) * valid
    key_feat = jax.nn.softplus(mixed[:, width : 2 * width]) * valid
    return (
        query_feat * cosine,
        query_feat * sine,
        key_feat * cosine,
        key_feat * sine,
        mixed[:, 2 * width :],
    )


def left_by_rows(left, right):
    return lax.dot_general(
        left, right, (((0,), (0,)), ((), ())), preferred_element_type=jnp.float32
    )


def right_by_rows(left, right):
    return lax.dot_general(
        left, right, (((1,), (1,)), ((), ())), preferred_element_type=jnp.float32
    )


def shards(
    tokens,
    lengths,
    weight_in,
    bias_in,
    weight_out,
    bias_out,
    gain_one,
    shift_one,
    weight_up,
    bias_up,
    weight_down,
    bias_down,
    gain_two,
    shift_two,
    cotangent,
):
    masters = (
        weight_in,
        bias_in,
        weight_out,
        bias_out,
        gain_one,
        shift_one,
        weight_up,
        bias_up,
        weight_down,
        bias_down,
        gain_two,
        shift_two,
    )
    lowered = [item.astype(jnp.bfloat16) for item in masters]
    full = (
        lax.all_gather(lowered[0], ("dp", "head"), axis=0, tiled=True),
        lax.all_gather(lowered[1], ("dp", "head"), axis=0, tiled=True),
        lax.all_gather(lowered[2], ("dp", "head"), axis=0, tiled=True),
        lax.all_gather(lowered[3], ("dp", "head"), axis=0, tiled=True),
        lax.all_gather(lowered[4], ("dp", "head"), axis=0, tiled=True),
        lax.all_gather(lowered[5], ("dp", "head"), axis=0, tiled=True),
        lax.all_gather(lowered[6], ("dp", "head"), axis=0, tiled=True),
        lax.all_gather(lowered[7], ("dp", "head"), axis=0, tiled=True),
        lax.all_gather(lowered[8], ("dp", "head"), axis=0, tiled=True),
        lax.all_gather(lowered[9], ("dp", "head"), axis=0, tiled=True),
        lax.all_gather(lowered[10], ("dp", "head"), axis=0, tiled=True),
        lax.all_gather(lowered[11], ("dp", "head"), axis=0, tiled=True),
    )
    proj_in, proj_out, proj_up, proj_down = (full[0], full[2], full[6], full[8])
    add_in = full[1].astype(jnp.float32)
    add_out = full[3].astype(jnp.float32)
    scale_one = full[4].astype(jnp.float32)
    offset_one = full[5].astype(jnp.float32)
    add_up = full[7].astype(jnp.float32)
    add_down = full[9].astype(jnp.float32)
    scale_two = full[10].astype(jnp.float32)
    offset_two = full[11].astype(jnp.float32)
    groups, local, width = tokens.shape
    parts = lax.axis_size("head")
    rows = groups * local
    length = local * parts
    head_width = width // parts
    per_device = head_width // HD
    inputs = tokens.reshape(rows, width)
    mixed = jnp.dot(inputs, proj_in, preferred_element_type=jnp.float32) + add_in
    places = (lax.axis_index("head") * local + jnp.arange(local)).astype(jnp.float32)
    limits = lengths.astype(jnp.float32)
    valid = (places[None, :] < limits[:, None]).astype(jnp.float32).reshape(rows, 1)
    angle = (0.5 * math.pi * places[None, :] / limits[:, None]).reshape(rows, 1)
    cosine = jnp.cos(angle)
    sine = jnp.sin(angle)
    feats, feat_pull = jax.vjp(lambda value: features(value, valid, cosine, sine), mixed)
    packed = jnp.stack(
        [item.astype(jnp.bfloat16).reshape(groups, local, parts, head_width) for item in feats],
        axis=3,
    )
    packed = packed.reshape(groups, local, parts, 5 * head_width)
    arrived = lax.all_to_all(packed, "head", split_axis=2, concat_axis=1, tiled=True)
    pieces = arrived.reshape(groups, length, 5, per_device, HD).astype(jnp.float32)
    attended, attend_pull = jax.vjp(
        partial(attend, block=BLOCK),
        pieces[:, :, 0],
        pieces[:, :, 1],
        pieces[:, :, 2],
        pieces[:, :, 3],
        pieces[:, :, 4],
    )
    sent = attended.astype(jnp.bfloat16).reshape(groups, length, 1, head_width)
    joined = lax.all_to_all(sent, "head", split_axis=1, concat_axis=2, tiled=True).reshape(
        rows, width
    )
    first = inputs.astype(jnp.float32) + (
        jnp.dot(joined, proj_out, preferred_element_type=jnp.float32) + add_out
    )
    normed, norm_one_pull = jax.vjp(norm, first, scale_one, offset_one)
    normed_low = normed.astype(jnp.bfloat16)
    upper = jnp.dot(normed_low, proj_up, preferred_element_type=jnp.float32) + add_up
    activated, gelu_pull = jax.vjp(partial(jax.nn.gelu, approximate=False), upper)
    hidden = activated.astype(jnp.bfloat16)
    second = normed + (jnp.dot(hidden, proj_down, preferred_element_type=jnp.float32) + add_down)
    result, norm_two_pull = jax.vjp(norm, second, scale_two, offset_two)
    activations = result.astype(jnp.bfloat16).reshape(groups, local, width)
    back_in, back_out, back_up, back_down = (proj_in, proj_out, proj_up, proj_down)
    seed = cotangent.reshape(rows, width).astype(jnp.float32)
    grad_second, grad_scale_two, grad_offset_two = norm_two_pull(seed)
    grad_branch = grad_second.astype(jnp.bfloat16)
    grad_proj_down = left_by_rows(hidden, grad_branch)
    grad_add_down = jnp.sum(grad_branch.astype(jnp.float32), axis=0)
    grad_hidden = right_by_rows(grad_branch, back_down)
    grad_upper = gelu_pull(grad_hidden)[0].astype(jnp.bfloat16)
    grad_proj_up = left_by_rows(normed_low, grad_upper)
    grad_add_up = jnp.sum(grad_upper.astype(jnp.float32), axis=0)
    grad_normed = grad_second + right_by_rows(grad_upper, back_up)
    grad_first, grad_scale_one, grad_offset_one = norm_one_pull(grad_normed)
    grad_out_branch = grad_first.astype(jnp.bfloat16)
    grad_proj_out = left_by_rows(joined, grad_out_branch)
    grad_add_out = jnp.sum(grad_out_branch.astype(jnp.float32), axis=0)
    grad_joined = right_by_rows(grad_out_branch, back_out).astype(jnp.bfloat16)
    grad_joined = grad_joined.reshape(groups, local, parts, head_width)
    grad_heads = lax.all_to_all(grad_joined, "head", split_axis=2, concat_axis=1, tiled=True)
    grad_heads = grad_heads.reshape(groups, length, per_device, HD).astype(jnp.float32)
    grad_feats = attend_pull(grad_heads)
    stacked = jnp.stack(
        [item.astype(jnp.bfloat16).reshape(groups, length, head_width) for item in grad_feats],
        axis=2,
    )
    stacked = stacked.reshape(groups, length, 1, 5 * head_width)
    returned = lax.all_to_all(stacked, "head", split_axis=1, concat_axis=2, tiled=True)
    unpacked = jnp.moveaxis(returned.reshape(groups, local, parts, 5, head_width), 3, 0)
    unpacked = unpacked.reshape(5, rows, width).astype(jnp.float32)
    grad_mixed = feat_pull((unpacked[0], unpacked[1], unpacked[2], unpacked[3], unpacked[4]))[
        0
    ].astype(jnp.bfloat16)
    grad_proj_in = left_by_rows(inputs, grad_mixed)
    grad_add_in = jnp.sum(grad_mixed.astype(jnp.float32), axis=0)
    grad_add_front = grad_add_in[: 2 * width]
    grad_add_value = grad_add_in[2 * width :]
    input_grad = (grad_first + right_by_rows(grad_mixed, back_in)).reshape(groups, local, width)
    ordered = (
        lax.psum_scatter(grad_proj_in, ("dp", "head"), scatter_dimension=0, tiled=True),
        lax.psum_scatter(grad_add_front, ("dp", "head"), scatter_dimension=0, tiled=True),
        lax.psum_scatter(grad_add_value, ("dp", "head"), scatter_dimension=0, tiled=True),
        lax.psum_scatter(grad_proj_out, ("dp", "head"), scatter_dimension=0, tiled=True),
        lax.psum_scatter(grad_add_out, ("dp", "head"), scatter_dimension=0, tiled=True),
        lax.psum_scatter(grad_scale_one, ("dp", "head"), scatter_dimension=0, tiled=True),
        lax.psum_scatter(grad_offset_one, ("dp", "head"), scatter_dimension=0, tiled=True),
        lax.psum_scatter(grad_proj_up, ("dp", "head"), scatter_dimension=0, tiled=True),
        lax.psum_scatter(grad_add_up, ("dp", "head"), scatter_dimension=0, tiled=True),
        lax.psum_scatter(grad_proj_down, ("dp", "head"), scatter_dimension=0, tiled=True),
        lax.psum_scatter(grad_add_down, ("dp", "head"), scatter_dimension=0, tiled=True),
        lax.psum_scatter(grad_scale_two, ("dp", "head"), scatter_dimension=0, tiled=True),
        lax.psum_scatter(grad_offset_two, ("dp", "head"), scatter_dimension=0, tiled=True),
    )
    return (
        activations,
        input_grad,
        ordered[0],
        ordered[1],
        ordered[2],
        ordered[3],
        ordered[4],
        ordered[5],
        ordered[6],
        ordered[7],
        ordered[8],
        ordered[9],
        ordered[10],
        ordered[11],
        ordered[12],
    )


def solution(mesh):
    placed = (
        P("dp", "head", None),
        P("dp"),
        P(("dp", "head"), None),
        P(("dp", "head")),
        P(("dp", "head"), None),
        P(("dp", "head")),
        P(("dp", "head")),
        P(("dp", "head")),
        P(("dp", "head"), None),
        P(("dp", "head")),
        P(("dp", "head"), None),
        P(("dp", "head")),
        P(("dp", "head")),
        P(("dp", "head")),
        P("dp", "head", None),
    )
    return jax.shard_map(
        shards,
        mesh=mesh,
        in_specs=placed,
        out_specs=(
            P("dp", "head", None),
            P("dp", "head", None),
            P(("dp", "head"), None),
            P(("dp", "head")),
            P(("dp", "head")),
            P(("dp", "head"), None),
            P(("dp", "head")),
            P(("dp", "head")),
            P(("dp", "head")),
            P(("dp", "head"), None),
            P(("dp", "head")),
            P(("dp", "head"), None),
            P(("dp", "head")),
            P(("dp", "head")),
            P(("dp", "head")),
        ),
        check_vma=False,
    )
```

profile of v0, /device:TPU:0, one launch (start us, length us, event | category | flops | bytes accessed | tf_op | source)
XLA Modules:
  0.0 2227.3 jit_solution(3295202175723201838)
XLA Ops:
  16.8 42.9 %all-reduce.21 = (bf16[2304]{0:T(1024)(128)(2,1)S(1)}, bf16[768]{0:T(1024)(128)(2,1)}, bf16[768]{0:T(1024)(128)(2,1)}, bf16[768]{0:T(1024)(128)(2,1)}, bf16[3072...) all-reduce(bf16[2304]{0:T(1024)(128)(2,1)S(1)} %dynamic-update-slic, ...), channel_id=1, replica_groups=mesh['dp'=8,'head'=4] {'dp','head'}, use_global_device_ids=true, to_apply=%add.3 | all-reduce | flops 9984 | bytes 39936
  59.7 14.6 all-gather.5.cloned.1.call-done
  74.4 8.4 convolution_add_fusion
  84.6 8.3 multiply_convert_fusion.1
  139.5 23.9 %copy.421 = bf16[3,512,4,5,192]{1,4,3,0,2:T(8,128)(2,1)} copy(bf16[3,512,4,5,192]{4,2,1,0,3:T(4,128)(2,1)} %constant_dynamic-update-slice_fusion) | data formatting | bytes 23592960 | tf_op jit(solution)/shard_map/reshape | solution.py:159
  171.3 260.9 %all-to-all-done = bf16[3,512,4,960]{1,3,0,2:T(8,128)(2,1)} async-done(((bf16[3,512,4,960]{1,3,0,2:T(8,128)(2,1)}), bf16[3,512,4,960]{1,3,0,2:T(8,128)(2,1)}, u32[]{:S(2)}, u32[]{:S(2)}) %all-to-all-start) | async-done | bytes 11796512 | tf_op jit(solution)/shard_map/all_to_all | solution.py:160
  432.2 25.8 %copy.328 = bf16[3,4,512,1,960]{2,1,4,0,3:T(4,128)(2,1)} copy(bf16[3,4,512,1,960]{2,4,0,1,3:T(8,128)(2,1)} %bitcast.4) | data formatting | bytes 23592960 | tf_op jit(solution)/shard_map/all_to_all | solution.py:160
  458.0 23.5 %reshape.299 = bf16[3,2048,5,3,64]{1,4,3,2,0:T(8,128)(2,1)} reshape(bf16[3,4,512,1,960]{2,1,4,0,3:T(4,128)(2,1)} %copy.328) | data formatting | bytes 23592960 | tf_op jit(solution)/shard_map/reshape | solution.py:161
  481.5 8.5 fusion.103
  497.6 8.0 reshape_squeeze.20
  513.2 8.0 reshape_squeeze.21
  521.1 7.9 reshape_squeeze.22
  529.1 8.0 reshape_squeeze.23
  537.1 8.9 reshape_squeeze.25
  552.4 8.8 reshape_squeeze.24
  587.9 10.8 fusion.75
  606.4 9.0 fusion.107
  630.6 8.1 copy.331
  638.8 13.5 sub.31
  652.2 13.4 sub.32
  665.6 14.2 fusion.104
  681.4 11.8 fusion.111
  693.2 12.1 fusion.112
  705.3 17.5 fusion.20
  722.8 10.2 copy.422
  733.1 15.6 reshape.334
  755.8 100.6 %all-to-all-done.1 = bf16[3,2048,1,192]{3,0,2,1:T(4,128)(2,1)} async-done(((bf16[3,2048,1,192]{3,0,2,1:T(4,128)(2,1)}), bf16[3,2048,1,192]{3,0,2,1:T(4,128)(2,1)}, u32[]{:S(2)}, u32[]{:S(2)}) %all-to-all-start.1) | async-done | bytes 2359328 | tf_op jit(solution)/shard_map/all_to_all | solution.py:171
  882.5 54.1 %multiply_convert_fusion = (bf16[1536,3072]{1,0:T(8,128)(2,1)}, f32[1536,3072]{1,0:T(8,128)}, f32[1536,3072]{1,0:T(8,128)}) fusion(f32[3072]{0:T(1024)S(1)} %convert_element_type.285, bf16[768,3072]{1,0:T(8,128)(2,1)} %all-gather.9.cloned.1.call-done, f32[1536,768]{1,0:T(8,128)} %copy-done.6, f32[768]{0:T(1024)S(1)} %convert_element_type.281, ...), kind=kOutput, calls=%fused_computation.4 | convolution fusion | flops 7565082624 | bytes 56653824 | tf_op jit(solution)/shard_map/dot_general | solution.py:179
  936.7 13.0 fusion.106
  959.6 26.8 %convert_reduce_fusion = (f32[3072]{0:T(1024)}, bf16[1536,3072]{1,0:T(8,128)(2,1)}) fusion(f32[1536,3072]{1,0:T(8,128)} %get-tuple-element.148, bf16[1536,768]{1,0:T(8,128)(2,1)} %get-tuple-element.136, bf16[3072,768]{1,0:T(8,128)(2,1)} %all-gather.11.cloned.1.call-done, f32[1536,3072]{1,0:T(8,128)} %get-tuple-element.178, f32[3072]{0:T(1024)S(1)} %convert_element_type.285), kind=kOutput, calls=%fused_computation.2 | convolution fusion | flops 7327970304 | bytes 54288384 | tf_op jit(solution)/shard_map/dot_general | solution.py:80
  986.4 13.7 multiply_reduce_fusion
  1029.8 15.0 fusion.93
  1044.8 32.5 %all-to-all-done.2 = bf16[3,512,4,192]{1,3,0,2:T(8,128)(2,1)S(1)} async-done(((bf16[3,512,4,192]{1,3,0,2:T(8,128)(2,1)}), bf16[3,512,4,192]{1,3,0,2:T(8,128)(2,1)S(1)}, u32[]{:S(2)}, u32[]{:S(2)}) %all-to-all-start.2) | async-done | bytes 2359328 | tf_op jit(solution)/shard_map/all_to_all | solution.py:202
  1083.2 8.7 reshape.307
  1091.9 15.0 fusion.16
  1106.9 14.1 fusion.21
  1121.2 14.0 fusion.25
  1135.3 11.1 fusion.24
  1146.4 19.0 fusion.12
  1165.5 17.7 fusion.10
  1192.2 13.2 fusion.110
  1205.5 14.1 fusion.59
  1219.6 15.5 fusion.58
  1235.1 12.9 fusion.109
  1248.0 14.1 fusion.57
  1262.1 17.8 fusion.56
  1279.9 22.8 %fusion.26 = bf16[3,32,64,3,64]{2,4,3,1,0:T(8,128)(2,1)} fusion(f32[3,32,3,64,64]{3,4,2,1,0:T(8,128)} %fusion.25, f32[3,32,3,64]{3,2,1,0:T(4,128)} %copy-done.32, f32[3,32,3,64]{3,2,1,0:T(4,128)S(1)} %bitcast_multiply_fusion.3, f32[3,32,3,64,64]{4,3,2,1,0:T(8,128)} %sub.31, f32[3,32,64,3,64]{2,1,4,3,0:T(8,128)} %reshape.307, f32[3,32,64,3]{2,3,1,0:T(4,128)S(1)} %copy-done.22), kind=kOutput, calls=%fused_computation.63 | convolution fusion | flops 911867904 | bytes 16736256 | tf_op jit(solution)/shard_map/transpose(jvp(bnihe,bnhef->bnihf))/dot_general | solution.py:42
  1302.7 23.0 %fusion.27 = bf16[3,32,64,3,64]{2,4,3,1,0:T(8,128)(2,1)} fusion(f32[3,32,3,64,64]{3,4,2,1,0:T(8,128)} %fusion.24, f32[3,32,3,64]{3,2,1,0:T(4,128)S(1)} %copy-done.31, f32[3,32,3,64]{3,2,1,0:T(4,128)S(1)} %bitcast_multiply_fusion.3, f32[3,32,3,64,64]{4,3,2,1,0:T(8,128)} %sub.32, f32[3,32,64,3,64]{2,1,4,3,0:T(8,128)} %reshape.307, ...), kind=kOutput, calls=%fused_computation.64 | convolution fusion | flops 911867904 | bytes 16736256 | tf_op jit(solution)/shard_map/transpose(jvp(bnihe,bnhef->bnihf))/dot_general | solution.py:43
  1326.2 15.3 fusion.7
  1341.5 27.9 %fusion.28 = bf16[3,32,64,3,64]{2,4,3,1,0:T(8,128)(2,1)} fusion(f32[3,32,3,64,64]{4,3,2,1,0:T(8,128)} %fusion.58, f32[3,32,3,64,64]{4,3,2,1,0:T(8,128)} %fusion.56, f32[3,32,3,64,64]{3,4,2,1,0:T(8,128)} %get-tuple-element.173, f32[3,32,64,3,64]{2,1,4,3,0:T(8,128)} %reshape.307, f32[3,32,64,3]{2,3,1,0:T(4,128)S(1)} %copy-done.22), kind=kOutput, calls=%fused_computation.65 | convolution fusion | flops 910688256 | bytes 21307392 | tf_op jit(solution)/shard_map/transpose(jvp(bnhij,bnjhe->bnihe))/dot_general | solution.py:32
  1369.4 15.0 fusion.6
  1422.3 8.0 convert_element_type.312
  1470.6 27.5 %copy.387 = bf16[3,2048,1,960]{3,0,2,1:T(4,128)(2,1)} copy(bf16[3,2048,1,960]{1,3,2,0:T(8,128)(2,1)} %bitcast.237) | data formatting | bytes 23592960 | tf_op jit(solution)/shard_map/reshape | solution.py:209
  1505.3 12.3 fusion.114
  1517.7 388.0 %all-to-all-done.3 = bf16[3,2048,1,960]{3,0,2,1:T(4,128)(2,1)} async-done(((bf16[3,2048,1,960]{3,0,2,1:T(4,128)(2,1)}), bf16[3,2048,1,960]{3,0,2,1:T(4,128)(2,1)}, u32[]{:S(2)}, u32[]{:S(2)}) %all-to-all-start.3) | async-done | bytes 11796512 | tf_op jit(solution)/shard_map/all_to_all | solution.py:210
  1905.7 25.1 %copy.388 = bf16[3,2048,1,960]{1,3,2,0:T(8,128)(2,1)} copy(bf16[3,2048,1,960]{3,0,2,1:T(4,128)(2,1)} %all-to-all-done.3) | data formatting | bytes 23592960 | tf_op jit(solution)/shard_map/all_to_all | solution.py:210
  1930.8 26.8 %reshape.310 = f32[3,4,512,1,960]{2,1,4,0,3:T(4,128)} reshape(bf16[3,2048,1,960]{1,3,2,0:T(8,128)(2,1)} %copy.388) | data formatting | bytes 35389440 | tf_op jit(solution)/shard_map/convert_element_type | solution.py:212
  1957.6 21.9 copy.389
  1979.5 14.7 fusion.101
  2068.6 14.0 fusion.34
  2094.7 8.1 copy.424
  2104.9 37.8 %all-reduce.20 = (f32[1536]{0:T(1024)S(1)}, f32[768]{0:T(1024)S(1)}, f32[768]{0:T(1024)S(1)}, f32[768]{0:T(1024)S(1)}, f32[768]{0:T(1024)S(1)}, /*index=5*/f32[3...) all-reduce(f32[1536]{0:T(1024)S(1)} %slice.87, ...), channel_id=3, replica_groups=mesh['dp'=8,'head'=4] {'dp','head'}, use_global_device_ids=true, to_apply=%region_22.24.clone | all-reduce | flops 9984 | bytes 79872
  2148.0 11.1 add_add_fusion.5
  2159.2 61.1 %reduce-scatter.13.cloned.1.call-done = f32[24,2304]{1,0:T(8,128)} async-done(((f32[768,2304]{1,0:T(8,128)}), f32[24,2304]{1,0:T(8,128)}) %reduce-scatter.13.cloned.1.call-update) | async-done | bytes 221200
  (354 shorter events, 405.5 us)
Async XLA Ops:
  7.2 67.2 %all-gather.5.cloned.1.call-start = ((), (), s32[]{:S(2)}) async-start(), calls=%async_computation.8 | async-start | bytes 3649536 | tf_op jit(solution)/shard_map/all_gather | solution.py:118
  14.9 69.7 %copy-start.33 = (f32[1536]{0:T(1024)}, f32[1536]{0:T(1024)S(1)}, u32[]{:S(2)}) copy-start(f32[1536]{0:T(1024)S(1)} %sin.12) | copy-start | bytes 18436
  15.0 69.6 %copy-start.35 = (f32[1536]{0:T(1024)}, f32[1536]{0:T(1024)S(1)}, u32[]{:S(2)}) copy-start(f32[1536]{0:T(1024)S(1)} %reshape.305) | copy-start | bytes 18436
  59.7 24.9 %copy-start.37 = (f32[1536]{0:T(1024)}, f32[1536]{0:T(1024)S(1)}, u32[]{:S(2)}) copy-start(f32[1536]{0:T(1024)S(1)} %cos.12) | copy-start | bytes 18436
  82.8 10.2 copy-start.3
  101.8 14.7 copy-start.11
  163.5 268.7 %all-to-all-start = ((bf16[3,512,4,960]{1,3,0,2:T(8,128)(2,1)}), bf16[3,512,4,960]{1,3,0,2:T(8,128)(2,1)}, u32[]{:S(2)}, u32[]{:S(2)}) async-start(bf16[3,512,4,960]{1,3,0,2:T(8,128)(2,1)} %bitcast.238), calls=%async_computation | async-start | bytes 23592960 | tf_op jit(solution)/shard_map/all_to_all | solution.py:160
  169.8 704.2 %all-gather.7.cloned.1.call-start = ((), (), s32[]{:S(2)}) async-start(), calls=%async_computation.9 | async-start | bytes 1216512 | tf_op jit(solution)/shard_map/all_gather | solution.py:120
  170.5 712.0 %all-gather.9.cloned.1.call-start = ((), (), s32[]{:S(2)}) async-start(), calls=%async_computation.10 | async-start | bytes 4866048 | tf_op jit(solution)/shard_map/all_gather | solution.py:124
  171.3 494.3 %copy-start.18 = (f32[64,64]{0,1:T(8,128)}, f32[64,64]{0,1:T(8,128)S(1)}, u32[]{:S(2)}) copy-start(f32[64,64]{0,1:T(8,128)S(1)} %fusion.88) | copy-start | bytes 49156
  481.5 11.2 copy-start.1
  552.4 73.3 %copy-start.30 = (f32[3,32,3,64]{3,2,1,0:T(4,128)}, f32[3,32,3,64]{3,2,1,0:T(4,128)S(1)}, u32[]{:S(2)}) copy-start(f32[3,32,3,64]{3,2,1,0:T(4,128)S(1)} %reduce-window_subtract_fusion) | copy-start | bytes 221188
  567.6 12.3 copy-start.32
  580.0 18.8 slice-start.5
  587.9 10.8 copy-start
  587.9 10.8 slice-start.6
  598.7 16.6 slice-start.9
  606.4 9.0 slice-start.10
  615.4 10.2 slice-start.20
  618.2 7.5 copy-start.2
  618.2 7.5 slice-start.21
  679.8 13.3 slice-start.17
  681.3 24.0 %copy-start.21 = (f32[3,32,64,3]{2,3,1,0:T(4,128)}, f32[3,32,64,3]{2,3,1,0:T(4,128)S(1)}, u32[]{:S(2)}) copy-start(f32[3,32,64,3]{2,3,1,0:T(4,128)S(1)} %maximum_bitcast_fusion) | copy-start | bytes 221188
  681.3 11.8 slice-start.18
  681.4 11.8 slice-start.19
  748.7 107.6 %all-to-all-start.1 = ((bf16[3,2048,1,192]{3,0,2,1:T(4,128)(2,1)}), bf16[3,2048,1,192]{3,0,2,1:T(4,128)(2,1)}, u32[]{:S(2)}, u32[]{:S(2)}) async-start(bf16[3,2048,1,192]{3,0,2,1:T(4,128)(2,1)} %reshape.334), calls=%async_computation.1 | async-start | bytes 8388608 | tf_op jit(solution)/shard_map/all_to_all | solution.py:171
  753.7 182.9 %all-gather.11.cloned.1.call-start = ((), (), s32[]{:S(2)}) async-start(), calls=%async_computation.11 | async-start | bytes 4866048 | tf_op jit(solution)/shard_map/all_gather | solution.py:126
  957.2 29.2 %slice-start.24 = ((s8[4718592]{0:T(1024)(128)(4,1)}), s8[4194304]{0:T(1024)(128)(4,1)S(1)}, s32[]{:S(2)}) async-start(s8[4718592]{0:T(1024)(128)(4,1)} %bitcast.245), calls=%async_computation.40 | async-start | bytes 8388608
  959.6 26.8 %slice-start.25 = ((s8[4718592]{0:T(1024)(128)(4,1)}), s8[524288]{0:T(1024)(128)(4,1)S(1)}, s32[]{:S(2)}) async-start(s8[4718592]{0:T(1024)(128)(4,1)} %bitcast.245), calls=%async_computation.41 | async-start | bytes 1048576
  986.4 13.7 copy-start.40
  1020.3 57.0 %all-to-all-start.2 = ((bf16[3,512,4,192]{1,3,0,2:T(8,128)(2,1)}), bf16[3,512,4,192]{1,3,0,2:T(8,128)(2,1)S(1)}, u32[]{:S(2)}, u32[]{:S(2)}) async-start(bf16[3,512,4,192]{1,3,0,2:T(8,128)(2,1)} %copy.351), calls=%async_computation.2 | async-start | bytes 4718592 | tf_op jit(solution)/shard_map/all_to_all | solution.py:202
  1023.9 1135.2 %reduce-scatter.7.cloned.1.call-start = ((), (), s32[]{:S(2)}) async-start(), calls=%async_computation.12 | async-start | bytes 2433024 | tf_op jit(solution)/shard_map/reduce_scatter | solution.py:225
  1029.8 1129.3 %reduce-scatter.9.cloned.1.call-start = ((), (), s32[]{:S(2)}) async-start(), calls=%async_computation.13 | async-start | bytes 9732096 | tf_op jit(solution)/shard_map/reduce_scatter | solution.py:229
  1083.2 8.7 copy-start.22
  1083.2 38.0 %slice-start.7 = ((s8[4718592]{0:T(1024)(128)(4,1)}), s8[524288]{0:T(1024)(128)(4,1)S(1)}, s32[]{:S(2)}) async-start(s8[4718592]{0:T(1024)(128)(4,1)} %bitcast.225), calls=%async_computation.23 | async-start | bytes 1048576
  1091.9 15.0 copy-start.25
  1091.9 29.2 %slice-start.8 = ((s8[4718592]{0:T(1024)(128)(4,1)}), s8[4194304]{0:T(1024)(128)(4,1)S(1)}, s32[]{:S(2)}) async-start(s8[4718592]{0:T(1024)(128)(4,1)} %bitcast.225), calls=%async_computation.24 | async-start | bytes 8388608
  1106.9 14.1 copy-start.24
  1106.9 14.3 copy-start.19
  1106.9 28.3 %slice-start.11 = ((s8[4718592]{0:T(1024)(128)(4,1)}), s8[524288]{0:T(1024)(128)(4,1)S(1)}, s32[]{:S(2)}) async-start(s8[4718592]{0:T(1024)(128)(4,1)} %bitcast.229), calls=%async_computation.27 | async-start | bytes 1048576
  1121.0 14.2 slice-start
  1121.2 14.1 slice-start.1
  1121.2 14.1 slice-start.2
  1121.2 14.1 slice-start.12
  1135.3 30.2 %slice-start.22 = ((s8[4718592]{0:T(1024)(128)(4,1)}), s8[524288]{0:T(1024)(128)(4,1)S(1)}, s32[]{:S(2)}) async-start(s8[4718592]{0:T(1024)(128)(4,1)} %bitcast.243), calls=%async_computation.38 | async-start | bytes 1048576
  1146.4 19.1 slice-start.23
  1146.4 36.8 %slice-start.15 = ((s8[4718592]{0:T(1024)(128)(4,1)}), s8[4194304]{0:T(1024)(128)(4,1)S(1)}, s32[]{:S(2)}) async-start(s8[4718592]{0:T(1024)(128)(4,1)} %bitcast.233), calls=%async_computation.31 | async-start | bytes 8388608
  1146.4 41.3 %slice-start.13 = ((s8[4718592]{0:T(1024)(128)(4,1)}), s8[4194304]{0:T(1024)(128)(4,1)S(1)}, s32[]{:S(2)}) async-start(s8[4718592]{0:T(1024)(128)(4,1)} %bitcast.231), calls=%async_computation.29 | async-start | bytes 8388608
  1165.5 17.7 slice-start.16
  1165.5 22.2 slice-start.14
  1183.3 22.2 slice-start.3
  1192.2 13.2 slice-start.4
  1279.9 22.8 %copy-start.31 = (f32[3,32,3,64]{3,2,1,0:T(4,128)S(1)}, f32[3,32,3,64]{3,2,1,0:T(4,128)}, u32[]{:S(2)}) copy-start(f32[3,32,3,64]{3,2,1,0:T(4,128)} %copy-done.30) | copy-start | bytes 221188
  1302.7 23.0 %copy-start.27 = (f32[3,32,3,1,64]{4,3,2,1,0:T(1,128)S(1)}, f32[3,32,3,1,64]{4,3,2,1,0:T(1,128)}, u32[]{:S(2)}) copy-start(f32[3,32,3,1,64]{4,3,2,1,0:T(1,128)} %fusion.86) | copy-start | bytes 221188
  1302.7 23.2 %copy-start.26 = (f32[3,32,3,1,64]{4,3,2,1,0:T(1,128)S(1)}, f32[3,32,3,1,64]{4,3,2,1,0:T(1,128)}, u32[]{:S(2)}) copy-start(f32[3,32,3,1,64]{4,3,2,1,0:T(1,128)} %fusion.84) | copy-start | bytes 221188
  1498.1 7.2 copy-start.20
  1498.1 407.5 %all-to-all-start.3 = ((bf16[3,2048,1,960]{3,0,2,1:T(4,128)(2,1)}), bf16[3,2048,1,960]{3,0,2,1:T(4,128)(2,1)}, u32[]{:S(2)}, u32[]{:S(2)}) async-start(bf16[3,2048,1,960]{3,0,2,1:T(4,128)(2,1)} %copy.387), calls=%async_computation.3 | async-start | bytes 33554432 | tf_op jit(solution)/shard_map/all_to_all | solution.py:210
  1505.3 653.9 %reduce-scatter.11.cloned.1.call-start = ((), (), s32[]{:S(2)}) async-start(), calls=%async_computation.14 | async-start | bytes 9732096 | tf_op jit(solution)/shard_map/reduce_scatter | solution.py:231
  1517.6 702.6 %reduce-scatter.13.cloned.1.call-start = ((), (), s32[]{:S(2)}) async-start(), calls=%async_computation.15 | async-start | bytes 7299072
  2060.8 7.8 copy-start.34
  2060.8 7.8 copy-start.36
  2060.8 7.8 copy-start.38
  2068.6 14.0 copy-start.8
  2102.8 45.2 %copy-start.44 = (f32[1536]{0:T(1024)S(1)}, f32[1536]{0:T(1024)}, u32[]{:S(2)}) copy-start(f32[1536]{0:T(1024)} %copy-done.43) | copy-start | bytes 18436
  (35 other events, 118.2 us)
Sparse Core Ops, SparseCore 0:
  11.4 62.9 all-gather.4
  174.0 259.8 all-gather.6
  437.3 60.9 all-gather.8
  757.0 122.0 all-gather.10
  1030.3 99.4 reduce-scatter.6
  1137.1 134.5 reduce-scatter.8
  1517.8 404.4 reduce-scatter.10
  2103.0 117.2 reduce-scatter.12
where the time goes:
time: 2240 us; the launch traced here: 2230 us
  waiting for transfers between devices  858 us (38%)
  local copies, waits for them, and re-layouts  591 us (26%)
  matrix products  516 us (23%)
  other arithmetic  144 us (6%)
  blocking collectives  80.8 us (4%)
    all_to_all x1, waiting for transfers between devices, shards(): lax.all_to_all(stacked, 'head', split_axis=1, concat_axis=2, tiled=True)  388 us
    all_to_all x1, waiting for transfers between devices, shards(): lax.all_to_all(packed, 'head', split_axis=2, concat_axis=1, tiled=True)  261 us
    all_to_all x1, waiting for transfers between devices, shards(): lax.all_to_all(sent, 'head', split_axis=1, concat_axis=2, tiled=True)  101 us
    unnamed x2, blocking collectives  80.8 us
    another operation x10, local copies, waits for them, and re-layouts, blocks(): return array.reshape(batch, count, block, heads, width)  79.2 us
    convert_element_type x10, local copies, waits for them, and re-layouts, shards(): item.astype(jnp.bfloat16).reshape(groups, length, head_width)  76.7 us
    unnamed x9, waiting for transfers between devices  61.3 us
    dot_general x3, matrix products, attend(): jnp.einsum('bnihe,bnhef->bnihf', query_sin, prior_sin, precision=highest)  58.2 us
  transfers between devices with their start and end apart: 12, of which 6 were waited for; matrix products, arithmetic and copies ran while one was open for 48% of the time, Pallas kernels for 0%

commit v1 on v0

v1 whole, which is shorter than its diff:
```python
import functools
import math

import jax
import jax.numpy as jnp
from jax import lax
from jax.experimental import pallas as pl
from jax.experimental.pallas import tpu as pltpu
from jax.sharding import PartitionSpec as P

F32 = jnp.float32
BF16 = jnp.bfloat16
CHUNK = 256
LANES = 128
HALF = 64
BIG = 60 * 1024 * 1024


def dot(a, b):
    return lax.dot_general(a, b, (((1,), (0,)), ((), ())), preferred_element_type=F32)


def dot_t(a, b):
    return lax.dot_general(a, b, (((1,), (1,)), ((), ())), preferred_element_type=F32)


def tdot(a, b):
    return lax.dot_general(a, b, (((0,), (0,)), ((), ())), preferred_element_type=F32)


def iota(shape, dim):
    return lax.broadcasted_iota(jnp.int32, shape, dim)


def block_mask(rows, cols):
    return ((iota((rows, cols), 0) & HALF) == (iota((rows, cols), 1) & HALF)).astype(F32)


def head_masks():
    lane = iota((1, LANES), 1)
    first = (lane < HALF).astype(F32)
    place = lane & (HALF - 1)
    return first, 1.0 - first, (place == 0).astype(F32), (place == 1).astype(F32)


def cos_poly(z):
    t = z * z
    r = -1.0 / 3628800 + t * (1.0 / 479001600)
    r = 1.0 / 40320 + t * r
    r = -1.0 / 720 + t * r
    r = 1.0 / 24 + t * r
    r = -0.5 + t * r
    return 1.0 + t * r


def sin_poly(z):
    t = z * z
    r = -1.0 / 39916800 + t * (1.0 / 6227020800)
    r = 1.0 / 362880 + t * r
    r = -1.0 / 5040 + t * r
    r = 1.0 / 120 + t * r
    r = -1.0 / 6 + t * r
    return z + z * (t * r)


def angles(start, limit, rows):
    place = iota((rows, LANES), 0) + start
    theta = jnp.minimum((0.5 * math.pi * place.astype(F32)) / limit.astype(F32), 0.5 * math.pi)
    return cos_poly(theta), sin_poly(theta), (place < limit).astype(F32)


def weights_within(limit):
    apart = iota((CHUNK, CHUNK), 0) - iota((CHUNK, CHUNK), 1)
    theta = jnp.minimum((0.5 * math.pi * apart.astype(F32)) / limit.astype(F32), 0.5 * math.pi)
    return jnp.where(apart >= 0, cos_poly(theta), 0.0)


def softplus(x):
    t = jnp.exp(-jnp.abs(x))
    tail = jnp.where(t < 1e-3, t * (1.0 - 0.5 * t), jnp.log(1.0 + t))
    return jnp.maximum(x, 0.0) + tail


def slope(feature):
    small = feature * (1.0 - feature * (0.5 - feature * (1.0 / 6)))
    return jnp.where(feature < 0.01, small, 1.0 - jnp.exp(-feature))


def pack(state):
    return jnp.concatenate(
        [state[0:64] + state[64:128], state[128:192] + state[192:256]], axis=0
    )


def unpack(packed, mask):
    top, bottom = packed[0:64], packed[64:128]
    return jnp.concatenate([top, top, bottom, bottom], axis=0) * mask


def spread(feature, cosine, sine):
    return jnp.concatenate([feature * cosine, feature * sine], axis=1).astype(BF16)


def stacked_heads(value, first, second):
    return jnp.concatenate([value * first, value * second], axis=0).astype(BF16)


def rows_of(s, c, local):
    return pl.ds(pl.multiple_of(s * local + c * CHUNK, CHUNK), CHUNK)


def lanes_of(p):
    return pl.ds(pl.multiple_of(p * LANES, LANES), LANES)


def mixed_kernel(groups, local, lens, tok, weight, bias, q_out, k_out, v_out, state_out, cos_s, sin_s, ok_s):
    width = tok.shape[1]
    pairs = width // LANES
    base = lax.axis_index("head") * local
    for s in range(groups):
        cosine, sine, valid = angles(base, lens[s], local)
        cos_s[s * local : (s + 1) * local] = cosine
        sin_s[s * local : (s + 1) * local] = sine
        ok_s[s * local : (s + 1) * local] = valid
    mask = block_mask(256, 256)
    ones = jnp.ones((CHUNK, LANES), BF16)

    def project(i, _):
        r = pl.ds(pl.multiple_of(i * CHUNK, CHUNK), CHUNK)
        x = tok[r]
        valid = ok_s[r]
        for part, out in enumerate((q_out, k_out)):
            for n in range(0, width, 256):
                at = part * width + n
                y = dot(x, weight[:, at : at + 256]) + bias[:, at : at + 256]
                out[r, n : n + 256] = (softplus(y) * jnp.concatenate([valid, valid], axis=1)).astype(BF16)
        for n in range(0, width, 256):
            at = 2 * width + n
            v_out[r, n : n + 256] = (dot(x, weight[:, at : at + 256]) + bias[:, at : at + 256]).astype(BF16)
        return 0

    lax.fori_loop(0, groups * local // CHUNK, project, 0)

    def sums(i, _):
        s, p = i // pairs, i % pairs
        total = jnp.zeros((256, 256), F32)
        for c in range(local // CHUNK):
            r, n = rows_of(s, c, local), lanes_of(p)
            k2 = spread(k_out[r, n].astype(F32), cos_s[r], sin_s[r])
            total = total + tdot(k2, jnp.concatenate([v_out[r, n], ones], axis=1))
        state_out[i] = pack(total * mask)
        return 0

    lax.fori_loop(0, groups * pairs, sums, 0)


def attend_kernel(
    groups, local, lens, q, k, v, prior, joined, rest, inverse, states, fine, cos_s, sin_s, within
):
    pairs = q.shape[1] // LANES
    base = lax.axis_index("head") * local
    for s in range(groups):
        cosine, sine, _ = angles(base, lens[s], local)
        cos_s[s * local : (s + 1) * local] = cosine
        sin_s[s * local : (s + 1) * local] = sine
        within[s] = weights_within(lens[s])
    count = local // CHUNK

    def body(i, _):
        s, p = i // pairs, i % pairs
        n = lanes_of(p)
        first, second, _, _ = head_masks()
        mask = block_mask(256, 256)
        ones = jnp.ones((CHUNK, LANES), BF16)
        state = unpack(prior[i].astype(F32), mask)
        for c in range(count):
            r = rows_of(s, c, local)
            cosine, sine = cos_s[r], sin_s[r]
            feature = q[r, n].astype(F32)
            key = k[r, n]
            value = jnp.concatenate([v[r, n], ones], axis=1)
            low = state.astype(BF16)
            states[i * count + c] = low
            fine[i * count + c] = (state - low.astype(F32)).astype(BF16)
            outer = dot(spread(feature, cosine, sine), low)
            scores = dot_t(stacked_heads(feature, first, second), key)
            m = within[s]
            scores = (scores * jnp.concatenate([m, m], axis=0)).astype(BF16)
            inner = dot(scores, value)
            both = outer + jnp.where(
                jnp.concatenate([first, first], axis=1) > 0, inner[:CHUNK], inner[CHUNK:]
            )
            den = both[:, LANES:]
            above = 1.0 / jnp.maximum(den, 1.0)
            attended = both[:, :LANES] * above
            rounded = attended.astype(BF16)
            joined[r, n] = rounded
            rest[r, n] = (attended - rounded.astype(F32)).astype(BF16)
            inverse[r, n] = jnp.where(den > 1.0, above, -1.0).astype(BF16)
            if c + 1 < count:
                state = state + tdot(spread(key.astype(F32), cosine, sine), value) * mask
        return 0

    lax.fori_loop(0, groups * pairs, body, 0)


def gelu_both(x):
    z = jnp.abs(x) * (1.0 / math.sqrt(2.0))
    t = 1.0 / (1.0 + 0.3275911 * z)
    e = jnp.exp(-0.5 * x * x)
    poly = t * (
        0.254829592 + t * (-0.284496736 + t * (1.421413741 + t * (-1.453152027 + t * 1.061405429)))
    )
    tail = 0.5 * poly * e
    phi = jnp.where(x >= 0, 1.0 - tail, tail)
    return x * phi, phi + x * e * (1.0 / math.sqrt(2.0 * math.pi))


def mean_of(x):
    return jnp.mean(x, axis=1, keepdims=True)


def column_sum(x):
    return jnp.sum(x, axis=0, keepdims=True)


def normalised(x):
    centred = x - mean_of(x)
    inv = lax.rsqrt(mean_of(centred * centred) + 1e-05)
    return centred * inv, inv


def feed_kernel(
    tok, joined, cot, w_out, w_up, w_down, b_out, g_one, s_one, b_up, b_down, g_two, s_two,
    act, g_first, g_joined, gw_out, gw_up, gw_down, gb_out, gg_one, gs_one, gb_up, gb_down, gg_two, gs_two,
    norm_s, low_s, hid_s, der_s, sec_s, branch_s, acc_s,
):
    rows = tok.shape[0]
    ff = w_up.shape[1]
    step = 768
    count = ff // step

    @pl.when(pl.program_id(0) == 0)
    def _():
        for ref in (gw_out, gw_up, gw_down, gb_out, gg_one, gs_one, gb_up, gb_down, gg_two, gs_two):
            ref[...] = jnp.zeros_like(ref)

    first = tok[...].astype(F32) + (dot(joined[...], w_out[...]) + b_out[...])
    unit_one, inv_one = normalised(first)
    norm_s[...] = unit_one
    normed = unit_one * g_one[...] + s_one[...]
    low_s[...] = normed.astype(BF16)
    sec_s[...] = normed + b_down[...]

    def up(j, _):
        n = pl.ds(pl.multiple_of(j * step, step), step)
        x = dot(low_s[...], w_up[:, n]) + b_up[:, n]
        y, d = gelu_both(x)
        hid_s[:, n] = y.astype(BF16)
        der_s[:, n] = d.astype(BF16)
        return 0

    lax.fori_loop(0, count, up, 0)
    second = sec_s[...] + dot(hid_s[...], w_down[...])
    unit_two, inv_two = normalised(second)
    act[...] = (unit_two * g_two[...] + s_two[...]).astype(BF16)
    c = cot[...].astype(F32)
    gg_two[...] += column_sum(c * unit_two)
    gs_two[...] += column_sum(c)
    e = c * g_two[...]
    g_second = inv_two * (e - mean_of(e) - unit_two * mean_of(e * unit_two))
    sec_s[...] = g_second
    branch = g_second.astype(BF16)
    branch_s[...] = branch
    gb_down[...] += column_sum(branch.astype(F32))

    def down(j, _):
        n = pl.ds(pl.multiple_of(j * step, step), step)
        gh = dot_t(branch_s[...], w_down[n, :])
        gu = gh * der_s[:, n].astype(F32)
        gu = gu.astype(BF16)
        der_s[:, n] = gu
        gb_up[:, n] += column_sum(gu.astype(F32))
        gw_down[n, :] += tdot(hid_s[:, n], branch_s[...])
        gw_up[:, n] += tdot(low_s[...], gu)
        return 0

    lax.fori_loop(0, count, down, 0)
    g_normed = sec_s[...] + dot_t(der_s[...], w_up[...])
    unit_one = norm_s[...]
    gg_one[...] += column_sum(g_normed * unit_one)
    gs_one[...] += column_sum(g_normed)
    e = g_normed * g_one[...]
    gf = inv_one * (e - mean_of(e) - unit_one * mean_of(e * unit_one))
    g_first[...] = gf
    go = gf.astype(BF16)
    gb_out[...] += column_sum(go.astype(F32))
    gw_out[...] += tdot(joined[...], go)
    g_joined[...] = dot_t(go, w_out[...]).astype(BF16)


def pulled(gj, joined, rest, inverse, one, two):
    ri = inverse.astype(F32)
    gnum = (gj.astype(F32) * jnp.abs(ri)).astype(BF16)
    product = gnum.astype(F32) * (joined.astype(F32) + rest.astype(F32))
    high = product.astype(BF16)
    low = (product - high.astype(F32)).astype(BF16)
    ones = block_mask(2 * LANES, LANES).astype(BF16)
    gden = jnp.where(ri > 0, -dot(jnp.concatenate([high, low], axis=1), ones), 0.0)
    high = gden.astype(BF16).astype(F32)
    return gnum, (high * one + (gden - high) * two).astype(BF16)


def later_kernel(groups, local, lens, q, gj, joined, rest, inverse, state_out, cos_s, sin_s):
    pairs = q.shape[1] // LANES
    base = lax.axis_index("head") * local
    for s in range(groups):
        cosine, sine, _ = angles(base, lens[s], local)
        cos_s[s * local : (s + 1) * local] = cosine
        sin_s[s * local : (s + 1) * local] = sine

    def body(i, _):
        s, p = i // pairs, i % pairs
        total = jnp.zeros((256, 256), F32)
        for c in range(local // CHUNK):
            r, n = rows_of(s, c, local), lanes_of(p)
            _, _, one, two = head_masks()
            gnum, gden = pulled(gj[r, n], joined[r, n], rest[r, n], inverse[r, n], one, two)
            q2 = spread(q[r, n].astype(F32), cos_s[r], sin_s[r])
            total = total + tdot(q2, jnp.concatenate([gnum, gden], axis=1))
        state_out[i] = pack(total * block_mask(256, 256))
        return 0

    lax.fori_loop(0, groups * pairs, body, 0)


def back_kernel(
    groups, local, lens, q, k, v, gj, joined, rest, inverse, states, fine, after, out, cos_s, sin_s, within
):
    width = q.shape[1]
    pairs = width // LANES
    count = local // CHUNK
    base = lax.axis_index("head") * local
    for s in range(groups):
        cosine, sine, _ = angles(base, lens[s], local)
        cos_s[s * local : (s + 1) * local] = cosine
        sin_s[s * local : (s + 1) * local] = sine
        within[s] = weights_within(lens[s])

    def body(i, _):
        s, p = i // pairs, i % pairs
        n = lanes_of(p)
        first, second, one, two = head_masks()
        mask = block_mask(256, 256)
        ones = jnp.ones((CHUNK, LANES), BF16)
        picks = jnp.broadcast_to(one + two, (CHUNK, LANES)).astype(BF16)
        state = unpack(after[i].astype(F32), mask)
        for c in reversed(range(count)):
            r = rows_of(s, c, local)
            cosine, sine = cos_s[r], sin_s[r]
            feature = q[r, n].astype(F32)
            key_low = k[r, n]
            key = key_low.astype(F32)
            value = v[r, n]
            gnum, gden = pulled(gj[r, n], joined[r, n], rest[r, n], inverse[r, n], one, two)
            m = within[s]
            m = jnp.concatenate([m, m], axis=0)
            q2 = spread(feature, cosine, sine)
            pair = jnp.concatenate([gnum, gden], axis=1)
            outer = dot_t(pair, states[i * count + c]) + dot_t(pair, fine[i * count + c])
            heads = stacked_heads(feature, first, second)
            scores = (dot_t(heads, key_low) * m).astype(BF16)
            gheads = stacked_heads(gnum.astype(F32), first, second)
            left = jnp.concatenate([gheads, stacked_heads(gden.astype(F32), first, second)], axis=1)
            g = (dot_t(left, jnp.concatenate([value, ones], axis=1)) * m).astype(BF16)
            inner = dot(g, key_low)
            gq = outer[:, :LANES] * cosine + outer[:, LANES:] * sine
            gq = gq + jnp.where(first > 0, inner[:CHUNK], inner[CHUNK:])
            low = state.astype(BF16)
            gv = dot(spread(key, cosine, sine), low[:, :LANES]) + tdot(gheads, scores).T
            pick = jnp.concatenate([value, picks], axis=1)
            outer = dot_t(pick, low) + dot_t(pick, (state - low.astype(F32)).astype(BF16))
            gk = outer[:, :LANES] * cosine + outer[:, LANES:] * sine + tdot(heads, g).T
            out[r, n] = (gq * slope(feature)).astype(BF16)
            out[r, pl.ds(pl.multiple_of(width + p * LANES, LANES), LANES)] = (gk * slope(key)).astype(BF16)
            out[r, pl.ds(pl.multiple_of(2 * width + p * LANES, LANES), LANES)] = gv.astype(BF16)
            if c > 0:
                state = state + tdot(q2, pair) * mask
        return 0

    lax.fori_loop(0, groups * pairs, body, 0)


def input_kernel(tok, gm, weight, g_first, grad, gw, gb):
    @pl.when(pl.program_id(0) == 0)
    def _():
        gw[...] = jnp.zeros_like(gw)
        gb[...] = jnp.zeros_like(gb)

    low = gm[...]
    gb[...] += column_sum(low.astype(F32))
    gw[...] += tdot(tok[...], low)
    grad[...] = g_first[...] + dot_t(low, weight[...])


VMEM = pl.BlockSpec(memory_space=pltpu.VMEM)
SMEM = pl.BlockSpec(memory_space=pltpu.SMEM)


def params():
    return pltpu.CompilerParams(vmem_limit_bytes=BIG)


def shape(dims, kind=BF16):
    return jax.ShapeDtypeStruct(dims, kind)


def shards(
    tokens, lengths, weight_in, bias_in, weight_out, bias_out, gain_one, shift_one,
    weight_up, bias_up, weight_down, bias_down, gain_two, shift_two, cotangent,
):
    groups, local, width = tokens.shape
    rows = groups * local
    pairs = width // LANES
    count = local // CHUNK
    axes = ("dp", "head")
    parts = lax.axis_size("head")
    me = lax.axis_index("head")

    def gather(item):
        return lax.all_gather(item.astype(BF16), axes, axis=0, tiled=True)

    w_in, w_out, w_up, w_down = map(gather, (weight_in, weight_out, weight_up, weight_down))
    small = (bias_in, bias_out, gain_one, shift_one, bias_up, bias_down, gain_two, shift_two)
    sizes = [item.shape[0] for item in small]
    gathered = lax.all_gather(jnp.concatenate([item.astype(BF16) for item in small]), axes, axis=0)
    cuts = [sum(sizes[:i]) for i in range(len(sizes) + 1)]
    b_in, b_out, g_one, s_one, b_up, b_down, g_two, s_two = (
        gathered[:, a:b].reshape(1, -1).astype(F32) for a, b in zip(cuts, cuts[1:])
    )
    ff = w_up.shape[1]
    tok = tokens.reshape(rows, width)
    table = pltpu.VMEM((rows, LANES), F32)
    plane = shape((rows, width))
    q, k, v, sums = pl.pallas_call(
        functools.partial(mixed_kernel, groups, local),
        out_shape=(plane, plane, plane, shape((groups * pairs, 128, 256), F32)),
        in_specs=[SMEM, VMEM, VMEM, VMEM],
        out_specs=(VMEM,) * 4,
        scratch_shapes=[table, table, table],
        compiler_params=params(),
    )(lengths, tok, w_in, b_in)

    def scanned(item, keep):
        every = lax.all_gather(item, "head", axis=0)
        use = keep(jnp.arange(parts)).astype(F32).reshape(parts, 1, 1, 1)
        return jnp.sum(every * use, axis=0)

    prior = scanned(sums, lambda at: at < me)
    joined, rest, inverse, states, fine = pl.pallas_call(
        functools.partial(attend_kernel, groups, local),
        out_shape=(plane,) * 3 + (shape((groups * pairs * count, 256, 256)),) * 2,
        in_specs=[SMEM] + [VMEM] * 4,
        out_specs=(VMEM,) * 5,
        scratch_shapes=[table, table, pltpu.VMEM((groups, CHUNK, CHUNK), F32)],
        compiler_params=params(),
    )(lengths, q, k, v, prior)

    tile = local

    def block(cols):
        return pl.BlockSpec((tile, cols), lambda i: (i, 0))

    def fixed(*dims):
        return pl.BlockSpec(dims, lambda i: (0,) * len(dims), pipeline_mode=pl.Buffered(1))

    vectors = [fixed(1, width)] * 3 + [fixed(1, ff)] + [fixed(1, width)] * 3
    weights = [fixed(width, width), fixed(width, ff), fixed(ff, width)]
    vector_shapes = [shape((1, width), F32)] * 3 + [shape((1, ff), F32)] + [shape((1, width), F32)] * 3
    (
        activations, g_first, g_joined, gw_out, gw_up, gw_down,
        gb_out, gg_one, gs_one, gb_up, gb_down, gg_two, gs_two,
    ) = pl.pallas_call(
        feed_kernel,
        grid=(rows // tile,),
        out_shape=[plane, shape((rows, width), F32), plane]
        + [shape((width, width), F32), shape((width, ff), F32), shape((ff, width), F32)]
        + vector_shapes,
        in_specs=[block(width)] * 3 + weights + vectors,
        out_specs=[block(width)] * 3 + weights + vectors,
        scratch_shapes=[
            pltpu.VMEM((tile, width), F32),
            pltpu.VMEM((tile, width), BF16),
            pltpu.VMEM((tile, ff), BF16),
            pltpu.VMEM((tile, ff), BF16),
            pltpu.VMEM((tile, width), F32),
            pltpu.VMEM((tile, width), BF16),
            pltpu.VMEM((8, LANES), F32),
        ],
        compiler_params=params(),
    )(
        tok, joined, cotangent.reshape(rows, width), w_out, w_up, w_down,
        b_out, g_one, s_one, b_up, b_down, g_two, s_two,
    )
    sums = pl.pallas_call(
        functools.partial(later_kernel, groups, local),
        out_shape=shape((groups * pairs, 128, 256), F32),
        in_specs=[SMEM] + [VMEM] * 5,
        out_specs=VMEM,
        scratch_shapes=[table, table],
        compiler_params=params(),
    )(lengths, q, g_joined, joined, rest, inverse)
    after = scanned(sums, lambda at: at > me)
    g_mixed = pl.pallas_call(
        functools.partial(back_kernel, groups, local),
        out_shape=shape((rows, 3 * width)),
        in_specs=[SMEM] + [VMEM] * 10,
        out_specs=VMEM,
        scratch_shapes=[table, table, pltpu.VMEM((groups, CHUNK, CHUNK), F32)],
        compiler_params=params(),
    )(lengths, q, k, v, g_joined, joined, rest, inverse, states, fine, after)
    input_grad, gw_in, gb_in = pl.pallas_call(
        input_kernel,
        grid=(rows // tile,),
        out_shape=[shape((rows, width), F32), shape((width, 3 * width), F32), shape((1, 3 * width), F32)],
        in_specs=[block(width), block(3 * width), fixed(width, 3 * width), block(width)],
        out_specs=[block(width), fixed(width, 3 * width), fixed(1, 3 * width)],
        compiler_params=params(),
    )(tok, g_mixed, w_in, g_first)

    def scatter(item):
        return lax.psum_scatter(item, axes, scatter_dimension=0, tiled=True)

    gb_in = gb_in.reshape(-1)
    cols = [gb_in[: 2 * width], gb_in[2 * width :]] + [
        item.reshape(-1) for item in (gb_out, gg_one, gs_one, gb_up, gb_down, gg_two, gs_two)
    ]
    total = lax.axis_size(axes)
    cut = [item.shape[0] // total for item in cols]
    merged = scatter(jnp.concatenate([item.reshape(total, -1) for item in cols], axis=1).reshape(-1))
    places = [sum(cut[:i]) for i in range(len(cut) + 1)]
    (gb_front, gb_value, gb_out, gg_one, gs_one, gb_up, gb_down, gg_two, gs_two) = (
        merged[a:b] for a, b in zip(places, places[1:])
    )
    return (
        activations.reshape(groups, local, width),
        input_grad.reshape(groups, local, width),
        scatter(gw_in), gb_front, gb_value, scatter(gw_out), gb_out, gg_one, gs_one,
        scatter(gw_up), gb_up, scatter(gw_down), gb_down, gg_two, gs_two,
    )


def solution(mesh):
    spread_rows = P("dp", "head", None)
    matrix = P(("dp", "head"), None)
    vector = P(("dp", "head"))
    return jax.shard_map(
        shards,
        mesh=mesh,
        in_specs=(
            spread_rows, P("dp"), matrix, vector, matrix, vector, vector, vector,
            matrix, vector, matrix, vector, vector, vector, spread_rows,
        ),
        out_specs=(
            spread_rows, spread_rows, matrix, vector, vector, matrix, vector, vector, vector,
            matrix, vector, matrix, vector, vector, vector,
        ),
        check_vma=False,
    )
```

time: 2240 us -> 1240 us (0.55)
  local copies, waits for them, and re-layouts: 591 us -> 9.76 us
  matrix products: 516 us -> 0 us
  Pallas kernels: 0 us -> 217 us
  other arithmetic: 144 us -> 22.8 us
  waiting for transfers between devices: 858 us -> 899 us
    all_to_all x4 -> x0, waiting for transfers between devices: 782 us -> none  [the longest x1 388 us: shards(): lax.all_to_all(stacked, 'head', split_axis=1, concat_axis=2, tiled=True)]
    dot_general x37 -> x0, matrix products: 516 us -> none  [the longest x3 58.2 us: attend(): jnp.einsum('bnihe,bnhef->bnihf', query_sin, prior_sin, precision=highest)]
    all_gather x4 -> x6, waiting for transfers between devices: 14.7 us -> 496 us  [the longest x2 322 us: scanned(): every = lax.all_gather(item, 'head', axis=0)]
    reduce_scatter x3 -> x4, waiting for transfers between devices: 0.02 us -> 401 us  [scatter(): return lax.psum_scatter(item, axes, scatter_dimension=0, tiled=True)]
    pallas_call x0 -> x6, Pallas kernels: none -> 217 us  [the longest x1 96 us: shards(): pl.pallas_call(feed_kernel, grid=(rows // tile,), out_shape=[plane, shape...]
    convert_element_type x17 -> x8, local copies, waits for them, and re-layouts: 165 us -> 5.43 us  [shards(): gathered[:, a:b].reshape(1, -1).astype(F32)]
    another operation x18 -> x7, local copies, waits for them, and re-layouts: 118 us -> 0.55 us  [shards(): item.reshape(total, -1)]
    reshape x6 -> x3, local copies, waits for them, and re-layouts: 88.4 us -> 0.26 us  [the longest x2 0.15 us: shards(): item.reshape(total, -1)]
  transfers between devices with their start and end apart: 12 -> 10, of which waited for: 6 -> 9; matrix products, arithmetic and copies ran while one was open for 48% -> 2% of each run, Pallas kernels for 0% -> 7%
where the time goes in v1:
time: 1240 us
  waiting for transfers between devices  899 us (72%)
  Pallas kernels  217 us (18%)
  blocking collectives  80.8 us (7%)
  other arithmetic  22.8 us (2%)
  between operations  14.5 us (1%)
    reduce_scatter x4, waiting for transfers between devices, scatter(): return lax.psum_scatter(item, axes, scatter_dimension=0, tiled=True)  401 us
    all_gather x2, waiting for transfers between devices, scanned(): every = lax.all_gather(item, 'head', axis=0)  322 us
    all_gather x4, waiting for transfers between devices, gather(): return lax.all_gather(item.astype(BF16), axes, axis=0, tiled=True)  174 us
    pallas_call x1, Pallas kernels, shards(): pl.pallas_call(feed_kernel, grid=(rows // tile,), out_shape=[plane, shape...  96 us
    unnamed x2, blocking collectives  80.8 us
    pallas_call x1, Pallas kernels, shards(): pl.pallas_call(functools.partial(back_kernel, groups, local), out_shape=s...  42 us
  transfers between devices with their start and end apart: 10, of which 9 were waited for; matrix products, arithmetic and copies ran while one was open for 2% of the time, Pallas kernels for 7%

profile of v1, /device:TPU:0, one launch (start us, length us, event | category | flops | bytes accessed | tf_op | source)
XLA Modules:
  0.0 1244.3 jit_solution(12405954838236343553)
XLA Ops:
  7.2 1.6 convert_element_type.90
  8.9 0.7 convert_element_type.91
  9.6 0.7 convert_element_type.92
  10.2 0.7 convert_element_type.93
  10.9 0.7 convert_element_type.94
  11.5 0.7 convert_element_type.95
  12.2 0.7 convert_element_type.96
  12.8 0.7 convert_element_type.97
  13.5 0.7 convert_element_type.98
  14.2 0.1 concatenate.6
  14.3 0.2 dynamic-update-slice
  14.5 42.3 %all-reduce = bf16[9984]{0:T(1024)(128)(2,1)S(1)} all-reduce(bf16[9984]{0:T(1024)(128)(2,1)S(1)} %dynamic-update-slice), channel_id=2, replica_groups=mesh['dp'=8,'head'=4] {'dp','head'}, use_global_device_ids=true, to_apply=%add | all-reduce | flops 9984 | bytes 39936
  56.8 0.1 reshape.203
  56.9 0.7 reshape.195.bias
  57.6 16.8 %all-gather.10.cloned.1.call-done.weight = bf16[768,2304]{1,0:T(8,128)(2,1)} async-done(((bf16[24,2304]{1,0:T(8,128)(2,1)}), bf16[768,2304]{1,0:T(8,128)(2,1)}) %all-gather.10.cloned.1.call-update) | async-done | bytes 3538960 | tf_op jit(solution)/shard_map/all_gather | solution.py:431
  74.4 21.3 %shard_map.262 = (bf16[1536,768]{1,0:T(8,128)(2,1)}, bf16[1536,768]{1,0:T(8,128)(2,1)}, bf16[1536,768]{1,0:T(8,128)(2,1)}, f32[18,128,256]{2,1,0:T(8,128)}) custom-call(s32[3]{0:T(128)} %lens.7, bf16[1536,768]{1,0:T(8,128)(2,1)} %bitcast.6, bf16[768,2304]{1,0:T(8,128)(2,1)} %all-gather.10.cloned.1.call-done.weight, f32[1,2304]{1,0:T(1,128)} %reshape.195.bias), custom_call_target="tpu_custom_call" | custom-call | tf_op jit(solution)/shard_map/pallas_call | solution.py:445
  95.8 0.6 convert_element_type.102
  96.5 0.7 convert_element_type.103
  97.3 0.7 convert_element_type.104
  98.0 0.1 slice_convert_fusion.3
  98.1 0.7 reshape.199.b_up
  98.8 0.1 slice_convert_fusion
  98.9 0.7 reshape.202.s_two
  99.6 0.7 reshape.201.g_two
  100.2 0.7 reshape.200.b_down
  100.9 0.7 reshape.198.s_one
  101.6 0.7 reshape.197.g_one
  102.3 0.7 reshape.196.b_out
  102.9 158.5 %all-gather.18.cloned.1.call-done = f32[72,128,256]{2,1,0:T(8,128)} async-done(((f32[18,128,256]{2,1,0:T(8,128)}), f32[72,128,256]{2,1,0:T(8,128)}) %all-gather.18.cloned.1.call-update) | async-done | bytes 9437200 | tf_op jit(solution)/shard_map/all_gather | solution.py:455
  261.5 6.5 multiply_reduce_fusion.1.prior
  268.0 23.7 %shard_map.263 = (bf16[1536,768]{1,0:T(8,128)(2,1)}, bf16[1536,768]{1,0:T(8,128)(2,1)}, bf16[1536,768]{1,0:T(8,128)(2,1)}, bf16[36,256,256]{2,1,0:T(8,128)(2,1)}, bf16[36,256,256]{2,1,0:T(8,128)(2,1)}) custom-call(s32[3]{0:T(128)} %lens.7, bf16[1536,768]{1,0:T(8,128)(2,1)} %get-tuple-element.40.q, bf16[1536,768]{1,0:T(8,128)(2,1)} %get-tuple-element.41.k, ...), custom_call_target="tpu_custom_call" | custom-call | tf_op jit(solution)/shard_map/pallas_call | solution.py:460
  291.6 25.5 %all-gather.12.cloned.1.call-done.w_out = bf16[768,768]{1,0:T(8,128)(2,1)} async-done(((bf16[24,768]{1,0:T(8,128)(2,1)}), bf16[768,768]{1,0:T(8,128)(2,1)}) %all-gather.12.cloned.1.call-update) | async-done | bytes 1179664 | tf_op jit(solution)/shard_map/all_gather | solution.py:431
  317.1 65.8 %all-gather.14.cloned.1.call-done.w_up = bf16[768,3072]{1,0:T(8,128)(2,1)} async-done(((bf16[24,3072]{1,0:T(8,128)(2,1)}), bf16[768,3072]{1,0:T(8,128)(2,1)}) %all-gather.14.cloned.1.call-update) | async-done | bytes 4718608 | tf_op jit(solution)/shard_map/all_gather | solution.py:431
  382.9 65.6 %all-gather.16.cloned.1.call-done.w_down = bf16[3072,768]{1,0:T(8,128)(2,1)} async-done(((bf16[96,768]{1,0:T(8,128)(2,1)}), bf16[3072,768]{1,0:T(8,128)(2,1)}) %all-gather.16.cloned.1.call-update) | async-done | bytes 4718608 | tf_op jit(solution)/shard_map/all_gather | solution.py:431
  448.5 96.0 %shard_map.264 = (bf16[1536,768]{1,0:T(8,128)(2,1)}, f32[1536,768]{1,0:T(8,128)}, bf16[1536,768]{1,0:T(8,128)(2,1)}, f32[768,768]{1,0:T(8,128)}, f32[768,3072]{1...) custom-call(bf16[1536,768]{1,0:T(8,128)(2,1)} %bitcast.7, ...), custom_call_target="tpu_custom_call" | custom-call | tf_op jit(solution)/shard_map/pallas_call | solution.py:483
  544.5 15.5 %shard_map.265 = f32[18,128,256]{2,1,0:T(8,128)} custom-call(s32[3]{0:T(128)} %lens.7, bf16[1536,768]{1,0:T(8,128)(2,1)} %get-tuple-element.40.q, bf16[1536,768]{1,0:T(8,128)(2,1)} %get-tuple-element.46.gj, bf16[1536,768]{1,0:T(8,128)(2,1)} %get-tuple-element.44.joined, bf16[1536,768]{1,0:T(8,128)(2,1)} %get-tuple-element.47.rest, ...), custom_call_target="tpu_custom_call" | custom-call | tf_op jit(solution)/shard_map/pallas_call | solution.py:505
  560.1 0.7 reduce-scatter.7.cloned.1.call-update
  560.8 0.7 reduce-scatter.9.cloned.1.call-update
  561.6 0.7 reduce-scatter.11.cloned.1.call-update
  562.3 163.5 %all-gather.20.cloned.1.call-done = f32[72,128,256]{2,1,0:T(8,128)} async-done(((f32[18,128,256]{2,1,0:T(8,128)}), f32[72,128,256]{2,1,0:T(8,128)}) %all-gather.20.cloned.1.call-update) | async-done | bytes 9437200 | tf_op jit(solution)/shard_map/all_gather | solution.py:455
  725.8 6.6 multiply_reduce_fusion.after
  732.3 42.0 %shard_map.266.gm = bf16[1536,2304]{1,0:T(8,128)(2,1)} custom-call(s32[3]{0:T(128)} %lens.7, bf16[1536,768]{1,0:T(8,128)(2,1)} %get-tuple-element.40.q, bf16[1536,768]{1,0:T(8,128)(2,1)} %get-tuple-element.41.k, bf16[1536,768]{1,0:T(8,128)(2,1)} %get-tuple-element.42.v, bf16[1536,768]{1,0:T(8,128)(2,1)} %get-tuple-element.46.gj, ...), custom_call_target="tpu_custom_call" | custom-call | tf_op jit(solution)/shard_map/pallas_call | solution.py:514
  774.3 18.8 %shard_map.267 = (f32[1536,768]{1,0:T(8,128)}, f32[768,2304]{1,0:T(8,128)}, f32[1,2304]{1,0:T(1,128)}) custom-call(bf16[1536,768]{1,0:T(8,128)(2,1)} %bitcast.8, bf16[1536,2304]{1,0:T(8,128)(2,1)} %shard_map.266.gm, bf16[768,2304]{1,0:T(8,128)(2,1)} %all-gather.10.cloned.1.call-done.weight, f32[1536,768]{1,0:T(8,128)} %get-tuple-element.51.g_first), custom_call_target="tpu_custom_call" | custom-call | tf_op jit(solution)/shard_map/pallas_call | solution.py:522
  793.2 0.6 copy-done.10
  793.9 0.5 broadcast.20
  794.5 0.7 reduce.13
  795.2 0.1 reshape_reshape.27
  795.3 0.1 reshape_reshape.26
  795.4 0.1 reshape_reshape.25
  795.5 0.1 reshape_reshape.23
  795.6 0.1 reshape_reshape.22
  795.6 0.1 reshape_reshape.21
  795.8 0.1 reshape.192
  795.9 0.1 reshape.193
  795.9 0.1 concatenate.7
  796.1 0.1 reshape.194
  796.2 38.5 %all-reduce.1 = f32[9984]{0:T(1024)S(1)} all-reduce(f32[9984]{0:T(1024)S(1)} %reshape.194), channel_id=6, replica_groups=mesh['dp'=8,'head'=4] {'dp','head'}, use_global_device_ids=true, to_apply=%region_3.0.clone | all-reduce | flops 9984 | bytes 79872
  834.7 0.1 dynamic-slice
  834.8 0.6 slice.74
  835.3 0.5 slice.69
  835.9 0.6 fusion
  836.5 134.7 %reduce-scatter.9.cloned.1.call-done = f32[24,3072]{1,0:T(8,128)} async-done(((f32[768,3072]{1,0:T(8,128)}), f32[24,3072]{1,0:T(8,128)}) %reduce-scatter.9.cloned.1.call-update) | async-done | bytes 294928 | tf_op jit(solution)/shard_map/reduce_scatter | solution.py:532
  971.1 141.1 %reduce-scatter.11.cloned.1.call-done = f32[96,768]{1,0:T(8,128)} async-done(((f32[3072,768]{1,0:T(8,128)}), f32[96,768]{1,0:T(8,128)}) %reduce-scatter.11.cloned.1.call-update) | async-done | bytes 294928 | tf_op jit(solution)/shard_map/reduce_scatter | solution.py:532
  1112.2 125.2 %reduce-scatter.5.cloned.1.call-done = f32[24,2304]{1,0:T(8,128)} async-done(((f32[768,2304]{1,0:T(8,128)}), f32[24,2304]{1,0:T(8,128)}) %reduce-scatter.5.cloned.1.call-update) | async-done | bytes 221200 | tf_op jit(solution)/shard_map/reduce_scatter | solution.py:532
  (52 shorter events, 0.8 us)
Async XLA Ops:
  7.2 67.2 %all-gather.10.cloned.1.call-start = ((), (), s32[]{:S(2)}) async-start(), calls=%async_computation.4 | async-start | bytes 3649536 | tf_op jit(solution)/shard_map/all_gather | solution.py:431
  8.8 252.6 %all-gather.18.cloned.1.call-start = ((), (), s32[]{:S(2)}) async-start(), calls=%async_computation.12 | async-start | bytes 11796480 | tf_op jit(solution)/shard_map/all_gather | solution.py:455
  74.4 21.4 %copy-start.2 = (f32[24,768]{1,0:T(8,128)S(1)}, f32[24,768]{1,0:T(8,128)}, u32[]{:S(2)}) copy-start(f32[24,768]{1,0:T(8,128)} %param.19) | copy-start | bytes 221188
  74.4 22.1 %copy-start = (f32[24,3072]{1,0:T(8,128)S(1)}, f32[24,3072]{1,0:T(8,128)}, u32[]{:S(2)}) copy-start(f32[24,3072]{1,0:T(8,128)} %param.23) | copy-start | bytes 884740
  74.4 22.9 %copy-start.1 = (f32[96,768]{1,0:T(8,128)S(1)}, f32[96,768]{1,0:T(8,128)}, u32[]{:S(2)}) copy-start(f32[96,768]{1,0:T(8,128)} %param.25) | copy-start | bytes 884740
  95.7 221.4 %all-gather.12.cloned.1.call-start = ((), (), s32[]{:S(2)}) async-start(), calls=%async_computation.5 | async-start | bytes 1216512 | tf_op jit(solution)/shard_map/all_gather | solution.py:431
  96.5 286.4 %all-gather.14.cloned.1.call-start = ((), (), s32[]{:S(2)}) async-start(), calls=%async_computation.6 | async-start | bytes 4866048 | tf_op jit(solution)/shard_map/all_gather | solution.py:431
  97.2 351.3 %all-gather.16.cloned.1.call-start = ((), (), s32[]{:S(2)}) async-start(), calls=%async_computation.7 | async-start | bytes 4866048 | tf_op jit(solution)/shard_map/all_gather | solution.py:431
  98.0 627.8 %all-gather.20.cloned.1.call-start = ((), (), s32[]{:S(2)}) async-start(), calls=%async_computation.13 | async-start | bytes 11796480 | tf_op jit(solution)/shard_map/all_gather | solution.py:455
  560.0 276.5 %reduce-scatter.7.cloned.1.call-start = ((), (), s32[]{:S(2)}) async-start(), calls=%async_computation.9 | async-start | bytes 2433024 | tf_op jit(solution)/shard_map/reduce_scatter | solution.py:532
  560.8 410.4 %reduce-scatter.9.cloned.1.call-start = ((), (), s32[]{:S(2)}) async-start(), calls=%async_computation.10 | async-start | bytes 9732096 | tf_op jit(solution)/shard_map/reduce_scatter | solution.py:532
  561.5 550.7 %reduce-scatter.11.cloned.1.call-start = ((), (), s32[]{:S(2)}) async-start(), calls=%async_computation.11 | async-start | bytes 9732096 | tf_op jit(solution)/shard_map/reduce_scatter | solution.py:532
  562.3 675.2 %reduce-scatter.5.cloned.1.call-start = ((), (), s32[]{:S(2)}) async-start(), calls=%async_computation.8 | async-start | bytes 7299072 | tf_op jit(solution)/shard_map/reduce_scatter | solution.py:532
  793.1 0.7 copy-start.10
  793.1 0.7 copy-start.9
  793.1 0.7 copy-start.8
  793.1 0.7 copy-start.7
  793.1 0.8 copy-start.6
  793.1 0.8 copy-start.5
  793.1 1.3 copy-start.3
  793.2 2.6 copy-start.4
Sparse Core Ops, SparseCore 0:
  11.4 62.9 all-gather.9
  95.8 165.5 all-gather.17
  264.8 52.2 all-gather.11
  320.4 62.4 all-gather.13
  386.1 62.3 all-gather.15
  560.1 165.5 all-gather.19
  731.6 97.3 reduce-scatter.6
  836.5 134.5 reduce-scatter.8
  977.6 134.5 reduce-scatter.10
  1119.3 118.1 reduce-scatter.4

commit v2 on v1

v2 whole, which is shorter than its diff:
```python
import functools
import math

import jax
import jax.numpy as jnp
from jax import lax
from jax.experimental import pallas as pl
from jax.experimental.pallas import tpu as pltpu
from jax.sharding import PartitionSpec as P

F32 = jnp.float32
BF16 = jnp.bfloat16
CHUNK = 256
LANES = 128
HALF = 64
BIG = 60 * 1024 * 1024
MESH = pl.DeviceIdType.MESH


def dot(a, b):
    return lax.dot_general(a, b, (((1,), (0,)), ((), ())), preferred_element_type=F32)


def dot_t(a, b):
    return lax.dot_general(a, b, (((1,), (1,)), ((), ())), preferred_element_type=F32)


def tdot(a, b):
    return lax.dot_general(a, b, (((0,), (0,)), ((), ())), preferred_element_type=F32)


def iota(shape, dim):
    return lax.broadcasted_iota(jnp.int32, shape, dim)


def block_mask(rows, cols):
    return ((iota((rows, cols), 0) & HALF) == (iota((rows, cols), 1) & HALF)).astype(F32)


def head_masks():
    lane = iota((1, LANES), 1)
    first = (lane < HALF).astype(F32)
    place = lane & (HALF - 1)
    return first, 1.0 - first, (place == 0).astype(F32), (place == 1).astype(F32)


def cos_poly(z):
    t = z * z
    r = -1.0 / 3628800 + t * (1.0 / 479001600)
    r = 1.0 / 40320 + t * r
    r = -1.0 / 720 + t * r
    r = 1.0 / 24 + t * r
    r = -0.5 + t * r
    return 1.0 + t * r


def sin_poly(z):
    t = z * z
    r = -1.0 / 39916800 + t * (1.0 / 6227020800)
    r = 1.0 / 362880 + t * r
    r = -1.0 / 5040 + t * r
    r = 1.0 / 120 + t * r
    r = -1.0 / 6 + t * r
    return z + z * (t * r)


def angles(start, limit, rows):
    place = iota((rows, LANES), 0) + start
    theta = jnp.minimum((0.5 * math.pi * place.astype(F32)) / limit.astype(F32), 0.5 * math.pi)
    return cos_poly(theta), sin_poly(theta), (place < limit).astype(F32)


def weights_within(limit):
    apart = iota((CHUNK, CHUNK), 0) - iota((CHUNK, CHUNK), 1)
    theta = jnp.minimum((0.5 * math.pi * apart.astype(F32)) / limit.astype(F32), 0.5 * math.pi)
    return jnp.where(apart >= 0, cos_poly(theta), 0.0)


def softplus(x):
    t = jnp.exp(-jnp.abs(x))
    tail = jnp.where(t < 1e-3, t * (1.0 - 0.5 * t), jnp.log(1.0 + t))
    return jnp.maximum(x, 0.0) + tail


def slope(feature):
    small = feature * (1.0 - feature * (0.5 - feature * (1.0 / 6)))
    return jnp.where(feature < 0.01, small, 1.0 - jnp.exp(-feature))


def pack(state):
    return jnp.concatenate([state[0:64] + state[64:128], state[128:192] + state[192:256]], axis=0)


def unpack(packed, mask):
    top, bottom = packed[0:64], packed[64:128]
    return jnp.concatenate([top, top, bottom, bottom], axis=0) * mask


def column_of(row, first):
    halves = []
    for at in (0, LANES):
        turned = jnp.broadcast_to(row[:, at : at + LANES], (LANES, LANES)).T
        halves.append(jnp.where(first > 0, turned[0:64], turned[64:128]))
    return jnp.concatenate(halves, axis=0)


def two_parts(state):
    high = state.astype(BF16)
    return jnp.concatenate([high, (state - high.astype(F32)).astype(BF16)], axis=1)


def twice(value):
    return jnp.concatenate([value, value], axis=1)


def spread(feature, cosine, sine):
    return jnp.concatenate([feature * cosine, feature * sine], axis=1).astype(BF16)


def stacked_heads(value, first, second):
    return jnp.concatenate([value * first, value * second], axis=0).astype(BF16)


def rows_of(s, c, local):
    return pl.ds(pl.multiple_of(s * local + c * CHUNK, CHUNK), CHUNK)


def lanes_of(p):
    return pl.ds(pl.multiple_of(p * LANES, LANES), LANES)


def fill_tables(groups, local, base, lens, cos_s, sin_s, ok_s, within):
    for s in range(groups):
        cosine, sine, valid = angles(base, lens[s], local)
        cos_s[s * local : (s + 1) * local] = cosine
        sin_s[s * local : (s + 1) * local] = sine
        if ok_s is not None:
            ok_s[s * local : (s + 1) * local] = valid
        within[s] = weights_within(lens[s])


def meet(targets):
    barrier = pltpu.get_barrier_semaphore()
    for target in targets:
        pl.semaphore_signal(barrier, inc=1, device_id=target, device_id_type=MESH)
    pl.semaphore_wait(barrier, len(targets))


class Chain:
    def __init__(self, step, pairs, refs):
        self.at, self.parts, self.pairs = lax.axis_index("head"), lax.axis_size("head"), pairs
        self.out_state, self.out_rows, self.in_state, self.in_rows, self.send, self.recv = refs
        self.before = {"head": lax.rem(self.at + self.parts - step, self.parts)}
        self.after = {"head": lax.rem(self.at + self.parts + step, self.parts)}
        last = self.parts - 1
        self.is_first = self.at == (0 if step > 0 else last)
        self.is_last = self.at == (last if step > 0 else 0)

    def copies(self, s):
        some = pl.ds(s * self.pairs, self.pairs)
        return [
            pltpu.make_async_remote_copy(
                src_ref=src.at[some], dst_ref=dst.at[some],
                send_sem=self.send.at[s, j], recv_sem=self.recv.at[s, j],
                device_id=self.after, device_id_type=MESH,
            )
            for j, (src, dst) in enumerate(
                ((self.out_state, self.in_state), (self.out_rows, self.in_rows))
            )
        ]

    def start(self, s):
        for copy in self.copies(s):
            copy.start()

    def arrive(self, s):
        for copy in self.copies(s):
            copy.wait_recv()

    def sent(self, s):
        for copy in self.copies(s):
            copy.wait_send()


def chain_scratch(groups, pairs):
    return [
        pltpu.VMEM((groups * pairs, 128, LANES), BF16),
        pltpu.VMEM((groups * pairs, 8, 256), F32),
        pltpu.VMEM((groups * pairs, 128, LANES), BF16),
        pltpu.VMEM((groups * pairs, 8, 256), F32),
        pltpu.SemaphoreType.DMA((groups, 2)),
        pltpu.SemaphoreType.DMA((groups, 2)),
    ]


def attend_kernel(
    groups, local, lens, tok, weight, bias,
    q, k, v, joined, rest, inverse, states, rows_out,
    cos_s, sin_s, ok_s, within, own, own_rows, part, part_rows, came, came_rows, num_s, den_s, *link,
):
    width = tok.shape[1]
    pairs = width // LANES
    count = local // CHUNK
    chain = Chain(1, pairs, link)
    meet([chain.before, chain.after])
    fill_tables(groups, local, chain.at * local, lens, cos_s, sin_s, ok_s, within)

    def project(i, _):
        r = pl.ds(pl.multiple_of(i * CHUNK, CHUNK), CHUNK)
        x = tok[r]
        valid = ok_s[r]
        for piece, out in enumerate((q, k)):
            for n in range(0, width, 256):
                m = piece * width + n
                y = dot(x, weight[:, m : m + 256]) + bias[:, m : m + 256]
                out[r, n : n + 256] = (softplus(y) * twice(valid)).astype(BF16)
        for n in range(0, width, 256):
            m = 2 * width + n
            v[r, n : n + 256] = (dot(x, weight[:, m : m + 256]) + bias[:, m : m + 256]).astype(BF16)
        return 0

    def sums(i, _):
        s, p = i // pairs, i % pairs
        mask = block_mask(256, LANES)
        total = jnp.zeros((256, LANES), F32)
        row = jnp.zeros((1, 256), F32)
        for c in range(count):
            r, n = rows_of(s, c, local), lanes_of(p)
            k2 = spread(k[r, n].astype(F32), cos_s[r], sin_s[r])
            total = total + tdot(k2, v[r, n])
            row = row + column_sum(k2.astype(F32))
            if c + 1 < count:
                part[i * (count - 1) + c] = pack(total * mask)
                part_rows[i * (count - 1) + c] = jnp.broadcast_to(row, (8, 256))
        own[i] = pack(total * mask)
        own_rows[i] = jnp.broadcast_to(row, (8, 256))
        came[i] = jnp.zeros((128, LANES), F32)
        came_rows[i] = jnp.zeros((8, 256), F32)
        return 0

    def arrive(s):
        chain.arrive(s)

        def one(p, _):
            i = s * pairs + p
            rows = chain.in_rows[i]
            column = column_of(rows[0:1], head_masks()[0])
            came[i] = chain.in_state[i].astype(F32) + column * rows[1:2, 0:LANES]
            came_rows[i] = rows
            return 0

        lax.fori_loop(0, pairs, one, 0)

    def leave(s):
        def one(p, _):
            i = s * pairs + p
            total = came[i] + own[i]
            row = came_rows[i][0:1] + own_rows[i][0:1]
            column = column_of(row, head_masks()[0])
            centre = column_sum(total) / jnp.maximum(column_sum(column), 1e-30)
            centre = centre.astype(BF16).astype(F32)
            chain.out_state[i] = (total - column * centre).astype(BF16)
            chain.out_rows[i] = jnp.concatenate([row, twice(centre), jnp.zeros((6, 256), F32)], axis=0)
            return 0

        lax.fori_loop(0, pairs, one, 0)
        chain.start(s)

    def intra(i, _):
        s, p = i // pairs, i % pairs
        n = lanes_of(p)
        first, second, _, _ = head_masks()
        ones = jnp.ones((CHUNK, LANES), BF16)
        m = within[s]
        m = jnp.concatenate([m, m], axis=0)
        for c in range(count):
            r = rows_of(s, c, local)
            scores = dot_t(stacked_heads(q[r, n].astype(F32), first, second), k[r, n])
            inner = dot((scores * m).astype(BF16), jnp.concatenate([v[r, n], ones], axis=1))
            both = jnp.where(twice(first) > 0, inner[:CHUNK], inner[CHUNK:])
            num_s[r, n] = both[:, :LANES]
            den_s[r, n] = both[:, LANES:]
        return 0

    def inter(i, _):
        s, p = i // pairs, i % pairs
        n = lanes_of(p)
        mask = block_mask(256, LANES)
        ones = block_mask(LANES, LANES).astype(BF16)
        for c in range(count):
            r = rows_of(s, c, local)
            state, row = came[i], came_rows[i][0:1]
            if c > 0:
                state = state + part[i * (count - 1) + c - 1]
                row = row + part_rows[i * (count - 1) + c - 1][0:1]
            state = two_parts(unpack(state, mask))
            states[i * count + c] = state
            rows_out[i * count + c] = jnp.broadcast_to(row, (8, 256))
            q2 = spread(q[r, n].astype(F32), cos_s[r], sin_s[r])
            both = dot(q2, state)
            num = both[:, :LANES] + both[:, LANES:] + num_s[r, n]
            weighed = q2.astype(F32) * row
            weighed = (weighed[:, :LANES] + weighed[:, LANES:]).astype(BF16)
            den = dot(weighed, ones) + den_s[r, n]
            above = 1.0 / jnp.maximum(den, 1.0)
            attended = num * above
            rounded = attended.astype(BF16)
            joined[r, n] = rounded
            rest[r, n] = (attended - rounded.astype(F32)).astype(BF16)
            inverse[r, n] = jnp.where(den > 1.0, above, -1.0).astype(BF16)
        return 0

    lax.fori_loop(0, groups * count, project, 0)
    lax.fori_loop(0, groups * pairs, sums, 0)

    @pl.when(chain.is_first)
    def _():
        for s in range(groups):
            leave(s)

    lax.fori_loop(0, groups * pairs, intra, 0)

    @pl.when(jnp.logical_not(chain.is_first))
    def _():
        for s in range(groups):
            arrive(s)

            @pl.when(jnp.logical_not(chain.is_last))
            def _():
                leave(s)

    lax.fori_loop(0, groups * pairs, inter, 0)

    @pl.when(jnp.logical_not(chain.is_last))
    def _():
        for s in range(groups):
            chain.sent(s)


def gelu_both(x):
    z = jnp.abs(x) * (1.0 / math.sqrt(2.0))
    t = 1.0 / (1.0 + 0.3275911 * z)
    e = jnp.exp(-0.5 * x * x)
    poly = t * (
        0.254829592 + t * (-0.284496736 + t * (1.421413741 + t * (-1.453152027 + t * 1.061405429)))
    )
    tail = 0.5 * poly * e
    phi = jnp.where(x >= 0, 1.0 - tail, tail)
    return x * phi, phi + x * e * (1.0 / math.sqrt(2.0 * math.pi))


def mean_of(x):
    return jnp.mean(x, axis=1, keepdims=True)


def column_sum(x):
    return jnp.sum(x, axis=0, keepdims=True)


def normalised(x):
    centred = x - mean_of(x)
    inv = lax.rsqrt(mean_of(centred * centred) + 1e-05)
    return centred * inv, inv


def feed_kernel(
    tok, joined, cot, w_out, w_up, w_down, b_out, g_one, s_one, b_up, b_down, g_two, s_two,
    act, g_first, g_joined, gw_out, gw_up, gw_down, gb_out, gg_one, gs_one, gb_up, gb_down, gg_two, gs_two,
    norm_s, low_s, hid_s, der_s, sec_s, branch_s, acc_s,
):
    rows = tok.shape[0]
    ff = w_up.shape[1]
    step = 768
    count = ff // step

    @pl.when(pl.program_id(0) == 0)
    def _():
        for ref in (gw_out, gw_up, gw_down, gb_out, gg_one, gs_one, gb_up, gb_down, gg_two, gs_two):
            ref[...] = jnp.zeros_like(ref)

    first = tok[...].astype(F32) + (dot(joined[...], w_out[...]) + b_out[...])
    unit_one, inv_one = normalised(first)
    norm_s[...] = unit_one
    normed = unit_one * g_one[...] + s_one[...]
    low_s[...] = normed.astype(BF16)
    sec_s[...] = normed + b_down[...]

    def up(j, _):
        n = pl.ds(pl.multiple_of(j * step, step), step)
        x = dot(low_s[...], w_up[:, n]) + b_up[:, n]
        y, d = gelu_both(x)
        hid_s[:, n] = y.astype(BF16)
        der_s[:, n] = d.astype(BF16)
        return 0

    lax.fori_loop(0, count, up, 0)
    second = sec_s[...] + dot(hid_s[...], w_down[...])
    unit_two, inv_two = normalised(second)
    act[...] = (unit_two * g_two[...] + s_two[...]).astype(BF16)
    c = cot[...].astype(F32)
    gg_two[...] += column_sum(c * unit_two)
    gs_two[...] += column_sum(c)
    e = c * g_two[...]
    g_second = inv_two * (e - mean_of(e) - unit_two * mean_of(e * unit_two))
    sec_s[...] = g_second
    branch = g_second.astype(BF16)
    branch_s[...] = branch
    gb_down[...] += column_sum(branch.astype(F32))

    def down(j, _):
        n = pl.ds(pl.multiple_of(j * step, step), step)
        gh = dot_t(branch_s[...], w_down[n, :])
        gu = gh * der_s[:, n].astype(F32)
        gu = gu.astype(BF16)
        der_s[:, n] = gu
        gb_up[:, n] += column_sum(gu.astype(F32))
        gw_down[n, :] += tdot(hid_s[:, n], branch_s[...])
        gw_up[:, n] += tdot(low_s[...], gu)
        return 0

    lax.fori_loop(0, count, down, 0)
    g_normed = sec_s[...] + dot_t(der_s[...], w_up[...])
    unit_one = norm_s[...]
    gg_one[...] += column_sum(g_normed * unit_one)
    gs_one[...] += column_sum(g_normed)
    e = g_normed * g_one[...]
    gf = inv_one * (e - mean_of(e) - unit_one * mean_of(e * unit_one))
    g_first[...] = gf
    go = gf.astype(BF16)
    gb_out[...] += column_sum(go.astype(F32))
    gw_out[...] += tdot(joined[...], go)
    g_joined[...] = dot_t(go, w_out[...]).astype(BF16)


def back_kernel(
    groups, local, lens, q, k, v, gj, joined, rest, inverse, states, rows_in, out,
    cos_s, sin_s, within, own, own_rows, part, part_rows, came, came_rows, gnum_s, gden_s, lane_s, *link,
):
    width = q.shape[1]
    pairs = width // LANES
    count = local // CHUNK
    chain = Chain(-1, pairs, link)
    meet([chain.before, chain.after])
    fill_tables(groups, local, chain.at * local, lens, cos_s, sin_s, None, within)

    def sums(i, _):
        s, p = i // pairs, i % pairs
        n = lanes_of(p)
        _, _, one, two = head_masks()
        mask = block_mask(256, LANES)
        ones = block_mask(2 * LANES, LANES).astype(BF16)
        total = jnp.zeros((256, LANES), F32)
        row = jnp.zeros((1, 256), F32)
        for c in reversed(range(count)):
            r = rows_of(s, c, local)
            ri = inverse[r, n].astype(F32)
            gnum = (gj[r, n].astype(F32) * jnp.abs(ri)).astype(BF16)
            product = gnum.astype(F32) * (joined[r, n].astype(F32) + rest[r, n].astype(F32))
            gden = jnp.where(ri > 0, -dot(two_parts(product), ones), 0.0)
            high = gden.astype(BF16).astype(F32)
            gnum_s[r, n] = gnum
            gden_s[r, n] = gden
            lane_s[r, n] = (high * one + (gden - high) * two).astype(BF16)
            q2 = spread(q[r, n].astype(F32), cos_s[r], sin_s[r])
            total = total + tdot(q2, gnum)
            row = row + column_sum(q2.astype(F32) * twice(gden))
            if c > 0:
                part[i * (count - 1) + c - 1] = pack(total * mask)
                part_rows[i * (count - 1) + c - 1] = jnp.broadcast_to(row, (8, 256))
        own[i] = pack(total * mask)
        own_rows[i] = jnp.broadcast_to(row, (8, 256))
        came[i] = jnp.zeros((128, LANES), F32)
        came_rows[i] = jnp.zeros((8, 256), F32)
        return 0

    def arrive(s):
        chain.arrive(s)

        def one(p, _):
            i = s * pairs + p
            came[i] = chain.in_state[i].astype(F32)
            came_rows[i] = chain.in_rows[i]
            return 0

        lax.fori_loop(0, pairs, one, 0)

    def leave(s):
        def one(p, _):
            i = s * pairs + p
            n = lanes_of(p)
            total = came[i] + own[i]
            low = total.astype(BF16)
            chain.out_state[i] = low
            lost = unpack(total - low.astype(F32), block_mask(256, LANES)).astype(BF16)
            mean = column_sum(v[pl.ds(s * local, local), n].astype(F32)) * (1.0 / local)
            row = dot_t(jnp.broadcast_to(mean, (8, LANES)).astype(BF16), lost)
            chain.out_rows[i] = came_rows[i] + own_rows[i] + row
            return 0

        lax.fori_loop(0, pairs, one, 0)
        chain.start(s)

    def main(i, _):
        s, p = i // pairs, i % pairs
        n = lanes_of(p)
        first, second, one, two = head_masks()
        mask = block_mask(256, LANES)
        ones = jnp.ones((CHUNK, LANES), BF16)
        m = within[s]
        m = jnp.concatenate([m, m], axis=0)
        for c in range(count):
            r = rows_of(s, c, local)
            cosine, sine = cos_s[r], sin_s[r]
            feature, key, value = q[r, n].astype(F32), k[r, n], v[r, n]
            gnum, gden, lane = gnum_s[r, n], gden_s[r, n], lane_s[r, n].astype(F32)
            row = rows_in[i * count + c][0:1]
            outer = dot_t(twice(gnum), states[i * count + c]) + twice(gden) * row
            gq = outer[:, :LANES] * cosine + outer[:, LANES:] * sine
            heads = stacked_heads(feature, first, second)
            scores = (dot_t(heads, key) * m).astype(BF16)
            gheads = stacked_heads(gnum.astype(F32), first, second)
            left = jnp.concatenate([gheads, stacked_heads(lane, first, second)], axis=1)
            g = (dot_t(left, jnp.concatenate([value, ones], axis=1)) * m).astype(BF16)
            inner = dot(g, key)
            gq = gq + jnp.where(first > 0, inner[:CHUNK], inner[CHUNK:])
            state, row = came[i], came_rows[i][0:1]
            if c + 1 < count:
                state = state + part[i * (count - 1) + c]
                row = row + part_rows[i * (count - 1) + c][0:1]
            state = two_parts(unpack(state, mask))
            k2 = spread(key.astype(F32), cosine, sine)
            gv = dot(k2, state[:, :LANES]) + tdot(gheads, scores).T
            outer = dot_t(twice(value), state) + row
            gk = outer[:, :LANES] * cosine + outer[:, LANES:] * sine + tdot(heads, g).T
            out[r, n] = (gq * slope(feature)).astype(BF16)
            out[r, pl.ds(pl.multiple_of(width + p * LANES, LANES), LANES)] = (
                gk * slope(key.astype(F32))
            ).astype(BF16)
            out[r, pl.ds(pl.multiple_of(2 * width + p * LANES, LANES), LANES)] = gv.astype(BF16)
        return 0

    lax.fori_loop(0, groups * pairs, sums, 0)

    @pl.when(chain.is_first)
    def _():
        for s in range(groups):
            leave(s)

    @pl.when(jnp.logical_not(chain.is_first))
    def _():
        for s in range(groups):
            arrive(s)

            @pl.when(jnp.logical_not(chain.is_last))
            def _():
                leave(s)

    lax.fori_loop(0, groups * pairs, main, 0)

    @pl.when(jnp.logical_not(chain.is_last))
    def _():
        for s in range(groups):
            chain.sent(s)


def input_kernel(tok, gm, weight, g_first, grad, gw, gb):
    @pl.when(pl.program_id(0) == 0)
    def _():
        gw[...] = jnp.zeros_like(gw)
        gb[...] = jnp.zeros_like(gb)

    low = gm[...]
    gb[...] += column_sum(low.astype(F32))
    gw[...] += tdot(tok[...], low)
    grad[...] = g_first[...] + dot_t(low, weight[...])


def peers():
    dp, z = lax.axis_index("dp"), lax.axis_index("head")
    core, x, y = lax.rem(dp, 2), lax.rem(dp // 2, 2), dp // 4
    twin = dp + 1 - 2 * core
    along_x, along_y = dp + 2 - 4 * x, dp + 4 - 8 * y
    one = along_x + core * (along_y - along_x)
    two = along_y + core * (along_x - along_y)
    return dp, z, twin, one, two, one + two - dp


class Copies:
    def __init__(self, send, recv):
        self.send, self.recv, self.all = send, recv, []

    def start(self, a, slot, src, dst, target):
        copy = pltpu.make_async_remote_copy(
            src_ref=src, dst_ref=dst, send_sem=self.send.at[a, slot], recv_sem=self.recv.at[a, slot],
            device_id=target, device_id_type=MESH,
        )
        copy.start()
        self.all.append(copy)
        return copy

    def finish(self):
        for copy in self.all:
            copy.wait_send()


class Gather:
    def __init__(self, ins, outs, local, send, recv):
        self.ins, self.outs, self.local = ins, outs, local
        self.copies, self.had = Copies(send, recv), {}
        self.dp, self.z, twin, one, two, self.far = peers()
        self.one, self.two = one, two
        self.to_z = [{"dp": self.dp, "head": lax.rem(self.z + k, 4)} for k in (1, 2, 3)]
        self.to_twin, self.to_one, self.to_two = (
            {"dp": d, "head": self.z} for d in (twin, one, two)
        )

    def targets(self):
        return self.to_z + [self.to_twin, self.to_one, self.to_two]

    def own(self, a):
        return pltpu.make_async_copy(self.ins[a], self.outs[a].at[self.dp * 4 + self.z], self.local.at[a])

    def begin(self, a):
        self.own(a).start()
        for k in range(3):
            place = self.outs[a].at[self.dp * 4 + self.z]
            self.had[a, k] = self.copies.start(a, k, self.ins[a], place, self.to_z[k])

    def pass_on(self, a, slot, block, target):
        ref = self.outs[a].at[pl.ds(block * 4, 4)]
        self.had[a, slot] = self.copies.start(a, slot, ref, ref, target)

    def stage(self, a, step):
        if step == 0:
            self.own(a).wait()
            for k in range(3):
                self.had[a, k].wait_recv()
            self.pass_on(a, 3, self.dp, self.to_one)
            self.pass_on(a, 4, self.dp, self.to_two)
            self.pass_on(a, 5, self.dp, self.to_twin)
        elif step == 1:
            self.had[a, 3].wait_recv()
            self.pass_on(a, 6, self.one, self.to_two)
            self.pass_on(a, 7, self.one, self.to_twin)
        elif step == 2:
            self.had[a, 4].wait_recv()
            self.pass_on(a, 8, self.two, self.to_twin)
        elif step == 3:
            self.had[a, 6].wait_recv()
            self.pass_on(a, 9, self.far, self.to_twin)
        elif step == 4:
            for slot in (5, 7, 8, 9):
                self.had[a, slot].wait_recv()

    def finish(self):
        self.copies.finish()


def gather_kernel(n, *refs):
    ins, outs = refs[:n], refs[n : 2 * n]
    work = Gather(ins, outs, *refs[2 * n :])
    meet(work.targets())
    for a in range(n):
        work.begin(a)
    for t in range(n + 4):
        for a in range(n):
            if 0 <= t - a < 5:
                work.stage(a, t - a)
    work.finish()


def gather_all(blocks):
    n = len(blocks)
    return pl.pallas_call(
        functools.partial(gather_kernel, n),
        out_shape=[shape((32,) + item.shape, item.dtype) for item in blocks],
        in_specs=[ANY] * n,
        out_specs=[ANY] * n,
        scratch_shapes=[
            pltpu.SemaphoreType.DMA((n,)),
            pltpu.SemaphoreType.DMA((n, 10)),
            pltpu.SemaphoreType.DMA((n, 10)),
        ],
        compiler_params=params(3),
    )(*blocks)


def folded(item):
    rows, cols = item.shape
    if rows % 16 == 0:
        return item
    return jnp.concatenate([item[:, : cols // 2], item[:, cols // 2 :]], axis=0)


def unfolded(item, rows):
    n, have, cols = item.shape
    if have == rows:
        return item.reshape(n * rows, cols)
    return item.reshape(n, 2, rows, cols).transpose(0, 2, 1, 3).reshape(n * rows, 2 * cols)


class Scatter:
    def __init__(self, bufs, boxes, outs, send, recv):
        self.bufs, self.boxes, self.outs = bufs, boxes, outs
        self.copies, self.had = Copies(send, recv), {}
        self.dp, self.z, self.twin, self.one, self.two, self.far = peers()
        self.to_z = [{"dp": self.dp, "head": lax.rem(self.z + k, 4)} for k in (1, 2, 3)]
        self.to_twin, self.to_one, self.to_two = (
            {"dp": d, "head": self.z} for d in (self.twin, self.one, self.two)
        )

    def targets(self):
        return self.to_z + [self.to_twin, self.to_one, self.to_two]

    def block(self, a, dp):
        return self.bufs[a].at[pl.ds(dp * 4, 4)]

    def begin(self, a):
        shift = self.twin - self.dp
        for slot, dp in enumerate((self.far, self.two, self.one, self.dp)):
            other = (self.far, self.one, self.two, self.dp)[slot] + shift
            self.had[a, slot] = self.copies.start(
                a, slot, self.block(a, other), self.boxes[a].at[pl.ds(slot * 4, 4)], self.to_twin
            )

    def add(self, a, dp, slots):
        buf, box = self.bufs[a], self.boxes[a]

        def one(j, _):
            total = buf[dp * 4 + j].astype(F32)
            for slot in slots:
                total = total + box[slot * 4 + j].astype(F32)
            buf[dp * 4 + j] = total.astype(BF16)
            return 0

        lax.fori_loop(0, 4, one, 0)

    def stage(self, a, step):
        box = self.boxes[a]
        if step == 0:
            self.had[a, 0].wait_recv()
            self.add(a, self.far, (0,))
            self.had[a, 4] = self.copies.start(a, 4, self.block(a, self.far), box.at[pl.ds(16, 4)], self.to_two)
            self.had[a, 1].wait_recv()
            self.add(a, self.two, (1,))
            self.had[a, 5] = self.copies.start(a, 5, self.block(a, self.two), box.at[pl.ds(20, 4)], self.to_two)
        elif step == 1:
            self.had[a, 2].wait_recv()
            self.had[a, 4].wait_recv()
            self.add(a, self.one, (2, 4))
            self.had[a, 6] = self.copies.start(a, 6, self.block(a, self.one), box.at[pl.ds(24, 4)], self.to_one)
        elif step == 2:
            for slot in (3, 5, 6):
                self.had[a, slot].wait_recv()
            self.add(a, self.dp, (3, 5, 6))
            for k in range(3):
                src = self.bufs[a].at[self.dp * 4 + lax.rem(self.z + k + 1, 4)]
                self.had[a, 7 + k] = self.copies.start(a, 7 + k, src, box.at[28 + k], self.to_z[k])
        elif step == 3:
            for k in range(3):
                self.had[a, 7 + k].wait_recv()
            total = self.bufs[a][self.dp * 4 + self.z].astype(F32)
            for k in range(3):
                total = total + box[28 + k].astype(F32)
            out = self.outs[a]
            rows, cols = total.shape
            if out.shape[0] == rows:
                out[...] = total
            else:
                out[:, :cols] = total[: rows // 2]
                out[:, cols:] = total[rows // 2 :]

    def finish(self):
        self.copies.finish()


class Total:
    def __init__(self, scatter, value, box, send, recv):
        self.value, self.box, self.to = value, box, scatter
        self.copies, self.had = Copies(send, recv), {}

    def pass_on(self, slot, target):
        self.had[slot] = self.copies.start(0, slot, self.value.at[slot if slot < 3 else 3], self.box.at[slot], target)

    def stage(self, step):
        value, box = self.value, self.box
        targets = (self.to.to_twin, self.to.to_two, self.to.to_one)
        if step > 0 and step < 4:
            self.had[step - 1].wait_recv()
            value[step] = value[step - 1] + box[step - 1]
        if step < 3:
            self.pass_on(step, targets[step])
        elif step == 3:
            for k in range(3):
                self.pass_on(3 + k, self.to.to_z[k])
        elif step == 4:
            for k in range(3):
                self.had[3 + k].wait_recv()
            value[4] = (value[3] + box[3]) + (box[4] + box[5])

    def finish(self):
        self.copies.finish()


def scatter_kernel(n, *refs):
    ins, small, outs, small_out = refs[:n], refs[n], refs[n + 1 : 2 * n + 1], refs[2 * n + 1]
    bufs, boxes = refs[2 * n + 2 : 3 * n + 2], refs[3 * n + 2 : 4 * n + 2]
    value, box, local, send, recv, small_send, small_recv = refs[4 * n + 2 :]
    work = Scatter(bufs, boxes, outs, send, recv)
    total = Total(work, value, box, small_send, small_recv)
    loads = [pltpu.make_async_copy(ins[a], bufs[a], local.at[a]) for a in range(n)]
    for load in loads:
        load.start()
    meet(work.targets())
    value[0] = small[...]
    for a in range(n):
        loads[a].wait()
        work.begin(a)
    for t in range(max(n + 3, 5)):
        if t < 5:
            total.stage(t)
        for a in range(n):
            if 0 <= t - a < 4:
                work.stage(a, t - a)
    small_out[...] = value[4]
    work.finish()
    total.finish()


def scatter_all(terms, small, places):
    n = len(terms)
    return pl.pallas_call(
        functools.partial(scatter_kernel, n),
        out_shape=[shape(place, F32) for place in places] + [shape(small.shape, F32)],
        in_specs=[ANY] * n + [VMEM],
        out_specs=[VMEM] * (n + 1),
        scratch_shapes=[pltpu.VMEM(item.shape, BF16) for item in terms]
        + [pltpu.VMEM((31,) + item.shape[1:], BF16) for item in terms]
        + [
            pltpu.VMEM((5,) + small.shape, F32),
            pltpu.VMEM((6,) + small.shape, F32),
            pltpu.SemaphoreType.DMA((n,)),
            pltpu.SemaphoreType.DMA((n, 10)),
            pltpu.SemaphoreType.DMA((n, 10)),
            pltpu.SemaphoreType.DMA((1, 6)),
            pltpu.SemaphoreType.DMA((1, 6)),
        ],
        compiler_params=params(4),
    )(*terms, small)


VMEM = pl.BlockSpec(memory_space=pltpu.VMEM)
SMEM = pl.BlockSpec(memory_space=pltpu.SMEM)
ANY = pl.BlockSpec(memory_space=pl.ANY)


def params(collective=None):
    if collective is None:
        return pltpu.CompilerParams(vmem_limit_bytes=BIG)
    return pltpu.CompilerParams(vmem_limit_bytes=BIG, collective_id=collective, has_side_effects=True)


def shape(dims, kind=BF16):
    return jax.ShapeDtypeStruct(dims, kind)


def shards(
    tokens, lengths, weight_in, bias_in, weight_out, bias_out, gain_one, shift_one,
    weight_up, bias_up, weight_down, bias_down, gain_two, shift_two, cotangent,
):
    groups, local, width = tokens.shape
    rows = groups * local
    pairs = width // LANES
    count = local // CHUNK
    axes = ("dp", "head")
    parts = lax.axis_size("head")
    me = lax.axis_index("head")

    by_kernel = lax.axis_size("dp") == 8 and parts == 4
    small = (bias_in, bias_out, gain_one, shift_one, bias_up, bias_down, gain_two, shift_two)
    if by_kernel:
        blocks = [folded(item.astype(BF16)) for item in (weight_in, weight_out, weight_up, weight_down)]
        slab = jnp.stack([jnp.pad(item.astype(BF16), (0, LANES - item.shape[0])) for item in small] * 2)
        *full, slabs = gather_all(blocks + [slab])
        w_in, w_out, w_up, w_down = (
            unfolded(item, own.shape[0])
            for item, own in zip(full, (weight_in, weight_out, weight_up, weight_down))
        )
        vectors = [slabs[:, j, : item.shape[0]] for j, item in enumerate(small)]
    else:

        def gather(item):
            return lax.all_gather(item.astype(BF16), axes, axis=0, tiled=True)

        w_in, w_out, w_up, w_down = map(gather, (weight_in, weight_out, weight_up, weight_down))
        sizes = [item.shape[0] for item in small]
        gathered = lax.all_gather(jnp.concatenate([item.astype(BF16) for item in small]), axes, axis=0)
        cuts = [sum(sizes[:i]) for i in range(len(sizes) + 1)]
        vectors = [gathered[:, a:b] for a, b in zip(cuts, cuts[1:])]
    b_in, b_out, g_one, s_one, b_up, b_down, g_two, s_two = (
        item.reshape(1, -1).astype(F32) for item in vectors
    )
    ff = w_up.shape[1]
    tok = tokens.reshape(rows, width)
    table = pltpu.VMEM((rows, LANES), F32)
    plane = shape((rows, width))
    units = groups * pairs

    def sums_scratch():
        return [
            pltpu.VMEM((units, 128, LANES), F32),
            pltpu.VMEM((units, 8, 256), F32),
            pltpu.VMEM((units * max(count - 1, 1), 128, LANES), F32),
            pltpu.VMEM((units * max(count - 1, 1), 8, 256), F32),
            pltpu.VMEM((units, 128, LANES), F32),
            pltpu.VMEM((units, 8, 256), F32),
        ]

    within = pltpu.VMEM((groups, CHUNK, CHUNK), F32)
    tall = pltpu.VMEM((rows, width), F32)
    q, k, v, joined, rest, inverse, states, state_rows = pl.pallas_call(
        functools.partial(attend_kernel, groups, local),
        out_shape=(plane,) * 6 + (shape((units * count, 256, 256)), shape((units * count, 8, 256), F32)),
        in_specs=[SMEM, VMEM, VMEM, VMEM],
        out_specs=(VMEM,) * 8,
        scratch_shapes=[table, table, table, within] + sums_scratch() + [tall, tall] + chain_scratch(groups, pairs),
        compiler_params=params(1),
    )(lengths, tok, w_in, b_in)

    tile = local

    def block(cols):
        return pl.BlockSpec((tile, cols), lambda i: (i, 0))

    def fixed(*dims):
        return pl.BlockSpec(dims, lambda i: (0,) * len(dims), pipeline_mode=pl.Buffered(1))

    vectors = [fixed(1, width)] * 3 + [fixed(1, ff)] + [fixed(1, width)] * 3
    weights = [fixed(width, width), fixed(width, ff), fixed(ff, width)]
    vector_shapes = [shape((1, width), F32)] * 3 + [shape((1, ff), F32)] + [shape((1, width), F32)] * 3
    (
        activations, g_first, g_joined, gw_out, gw_up, gw_down,
        gb_out, gg_one, gs_one, gb_up, gb_down, gg_two, gs_two,
    ) = pl.pallas_call(
        feed_kernel,
        grid=(rows // tile,),
        out_shape=[plane, shape((rows, width), F32), plane]
        + [shape((width, width), F32), shape((width, ff), F32), shape((ff, width), F32)]
        + vector_shapes,
        in_specs=[block(width)] * 3 + weights + vectors,
        out_specs=[block(width)] * 3 + weights + vectors,
        scratch_shapes=[
            pltpu.VMEM((tile, width), F32),
            pltpu.VMEM((tile, width), BF16),
            pltpu.VMEM((tile, ff), BF16),
            pltpu.VMEM((tile, ff), BF16),
            pltpu.VMEM((tile, width), F32),
            pltpu.VMEM((tile, width), BF16),
            pltpu.VMEM((8, LANES), F32),
        ],
        compiler_params=params(),
    )(
        tok, joined, cotangent.reshape(rows, width), w_out, w_up, w_down,
        b_out, g_one, s_one, b_up, b_down, g_two, s_two,
    )
    g_mixed = pl.pallas_call(
        functools.partial(back_kernel, groups, local),
        out_shape=shape((rows, 3 * width)),
        in_specs=[SMEM] + [VMEM] * 9,
        out_specs=VMEM,
        scratch_shapes=[table, table, within] + sums_scratch()
        + [pltpu.VMEM((rows, width), BF16), tall, pltpu.VMEM((rows, width), BF16)] + chain_scratch(groups, pairs),
        compiler_params=params(2),
    )(lengths, q, k, v, g_joined, joined, rest, inverse, states, state_rows)
    input_grad, gw_in, gb_in = pl.pallas_call(
        input_kernel,
        grid=(rows // tile,),
        out_shape=[shape((rows, width), F32), shape((width, 3 * width), F32), shape((1, 3 * width), F32)],
        in_specs=[block(width), block(3 * width), fixed(width, 3 * width), block(width)],
        out_specs=[block(width), fixed(width, 3 * width), fixed(1, 3 * width)],
        compiler_params=params(),
    )(tok, g_mixed, w_in, g_first)

    gb_in = gb_in.reshape(-1)
    cols = [gb_in[: 2 * width], gb_in[2 * width :]] + [
        item.reshape(-1) for item in (gb_out, gg_one, gs_one, gb_up, gb_down, gg_two, gs_two)
    ]
    total = lax.axis_size(axes)
    if by_kernel:
        terms = (gw_down, gw_up, gw_out, gw_in)
        places = [(item.shape[0] // 32, item.shape[1]) for item in terms]
        cut = []
        for item in terms:
            item = item.reshape(32, -1, item.shape[1])
            cut.append(jax.vmap(folded)(item).astype(BF16))
        flat = jnp.concatenate(cols).reshape(-1, width)
        flat = jnp.pad(flat, ((0, -flat.shape[0] % 8), (0, 0)))
        gw_down, gw_up, gw_out, gw_in, flat = scatter_all(cut, flat, places)
        flat = flat.reshape(-1)
        me = lax.axis_index(axes)
        mine, at = [], 0
        for item in cols:
            size = item.shape[0] // 32
            mine.append(lax.dynamic_slice(flat, (at + me * size,), (size,)))
            at += item.shape[0]
        gb_front, gb_value, gb_out, gg_one, gs_one, gb_up, gb_down, gg_two, gs_two = mine
        return (
            activations.reshape(groups, local, width),
            input_grad.reshape(groups, local, width),
            gw_in, gb_front, gb_value, gw_out, gb_out, gg_one, gs_one,
            gw_up, gb_up, gw_down, gb_down, gg_two, gs_two,
        )

    def scatter(item):
        return lax.psum_scatter(item, axes, scatter_dimension=0, tiled=True)

    cut = [item.shape[0] // total for item in cols]
    merged = scatter(jnp.concatenate([item.reshape(total, -1) for item in cols], axis=1).reshape(-1))
    places = [sum(cut[:i]) for i in range(len(cut) + 1)]
    (gb_front, gb_value, gb_out, gg_one, gs_one, gb_up, gb_down, gg_two, gs_two) = (
        merged[a:b] for a, b in zip(places, places[1:])
    )
    return (
        activations.reshape(groups, local, width),
        input_grad.reshape(groups, local, width),
        scatter(gw_in), gb_front, gb_value, scatter(gw_out), gb_out, gg_one, gs_one,
        scatter(gw_up), gb_up, scatter(gw_down), gb_down, gg_two, gs_two,
    )


def solution(mesh):
    spread_rows = P("dp", "head", None)
    matrix = P(("dp", "head"), None)
    vector = P(("dp", "head"))
    return jax.shard_map(
        shards,
        mesh=mesh,
        in_specs=(
            spread_rows, P("dp"), matrix, vector, matrix, vector, vector, vector,
            matrix, vector, matrix, vector, vector, vector, spread_rows,
        ),
        out_specs=(
            spread_rows, spread_rows, matrix, vector, vector, matrix, vector, vector, vector,
            matrix, vector, matrix, vector, vector, vector,
        ),
        check_vma=False,
    )
```

time: 1240 us -> 508 us (0.41); the launches traced: 1240 us -> 500 us
  waiting for transfers between devices: 899 us -> 0 us
  Pallas kernels: 217 us -> 425 us
  blocking collectives: 80.8 us -> 0 us
  local copies, waits for them, and re-layouts: 9.76 us -> 47.7 us
  between operations: 14.5 us -> 1.53 us
    all_gather x6 -> x0, waiting for transfers between devices: 496 us -> none  [the longest x2 322 us: scanned(): every = lax.all_gather(item, 'head', axis=0)]
    reduce_scatter x4 -> x0, waiting for transfers between devices: 401 us -> none  [scatter(): return lax.psum_scatter(item, axes, scatter_dimension=0, tiled=True)]
    pallas_call x2, Pallas kernels: 36.8 us -> 158 us  [the longest x1 81.3 us: gather_all(): pl.pallas_call(functools.partial(gather_kernel, n), out_shape=[shape((32,...]
    unnamed x2 -> x0, blocking collectives: 80.8 us -> none
    pallas_call x1, Pallas kernels: 42 us -> 98.8 us  [shards(): pl.pallas_call(functools.partial(back_kernel, groups, local), out_shape=s...]
    pallas_call x1, Pallas kernels: 23.7 us -> 52.9 us  [shards(): pl.pallas_call(functools.partial(attend_kernel, groups, local), out_shape...]
    unnamed x25 -> x47, local copies, waits for them, and re-layouts: 0.95 us -> 20.8 us
    reshape x3 -> x5, local copies, waits for them, and re-layouts: 0.26 us -> 15.7 us  [the longest x3 14.9 us: unfolded(): item.reshape(n, 2, rows, cols).transpose(0, 2, 1, 3)]
  transfers between devices with their start and end apart: 10 -> 0, of which waited for: 9 -> 0; matrix products, arithmetic and copies ran while one was open for 2% -> 0% of each run, Pallas kernels for 7% -> 0%
where the time goes in v2:
time: 508 us; the launch traced here: 500 us
  Pallas kernels  425 us (84%)
  local copies, waits for them, and re-layouts  47.7 us (9%)
  other arithmetic  25.9 us (5%)
    pallas_call x1, Pallas kernels, shards(): pl.pallas_call(functools.partial(back_kernel, groups, local), out_shape=s...  98.8 us
    pallas_call x1, Pallas kernels, shards(): pl.pallas_call(feed_kernel, grid=(rows // tile,), out_shape=[plane, shape...  96.1 us
    pallas_call x1, Pallas kernels, gather_all(): pl.pallas_call(functools.partial(gather_kernel, n), out_shape=[shape((32,...  81.3 us
    pallas_call x1, Pallas kernels, scatter_all(): pl.pallas_call(functools.partial(scatter_kernel, n), out_shape=[shape(pla...  77 us
    pallas_call x1, Pallas kernels, shards(): pl.pallas_call(functools.partial(attend_kernel, groups, local), out_shape...  52.9 us
    unnamed x47, local copies, waits for them, and re-layouts  20.8 us
    pallas_call x1, Pallas kernels, shards(): pl.pallas_call(input_kernel, grid=(rows // tile,), out_shape=[shape((rows...  18.5 us
    reshape x3, local copies, waits for them, and re-layouts, unfolded(): item.reshape(n, 2, rows, cols).transpose(0, 2, 1, 3)  14.9 us

profile of v2, /device:TPU:0, one launch (start us, length us, event | category | flops | bytes accessed | tf_op | source)
XLA Modules:
  0.0 499.8 jit_solution(818488475744141020)
XLA Ops:
  0.6 0.7 convert_element_type.107
  1.3 0.7 convert_element_type.108
  2.0 0.7 convert_element_type.105
  2.6 0.7 convert_element_type.106
  3.3 0.7 convert_element_type.103
  3.9 0.7 convert_element_type.104
  4.6 0.7 convert_element_type.101
  5.3 0.7 convert_element_type.102
  5.9 1.2 stack.43.refs_4_
  7.1 1.0 convert_element_type.99
  8.1 0.7 pad_maximum_fusion.3.refs_2_
  8.8 0.9 convert_element_type.97
  9.8 0.7 pad_maximum_fusion.4.refs_0_
  10.4 0.9 convert_element_type.98
  11.3 0.6 pad_maximum_fusion.5.refs_1_
  12.0 1.6 convert_element_type.100.refs_3_
  13.6 81.3 %shard_map.262 = (bf16[32,48,1152]{2,1,0:T(8,128)(2,1)}, bf16[32,48,384]{2,1,0:T(8,128)(2,1)}, bf16[32,48,1536]{2,1,0:T(8,128)(2,1)}, bf16[32,96,768]{2,1,0:T(8,128)(2,1)}, bf16[32,16,128]{2,1,0:T(8,128)(2,1)}) custom-call(bf16[48,1152]{1,0:T(8,128)(2,1)} %pad_maximum_fusion.4.refs_0_, bf16[48,384]{1,0:T(8,128)(2,1)} %pad_maximum_fusion.5.refs_1_, ...), custom_call_target="tpu_custom_call" | custom-call | tf_op jit(solution)/shard_map/pallas_call | solution.py:674
  94.9 0.9 convert_reduce_fusion.7
  95.8 0.7 reshape.239.bias
  96.5 4.7 copy.33
  101.2 2.3 copy.36
  103.6 52.9 %shard_map.263 = (bf16[1536,768]{1,0:T(8,128)(2,1)}, bf16[1536,768]{1,0:T(8,128)(2,1)}, bf16[1536,768]{1,0:T(8,128)(2,1)}, bf16[1536,768]{1,0:T(8,128)(2,1)}, bf...) custom-call(s32[3]{0:T(128)} %lens.3, ...), custom_call_target="tpu_custom_call" | custom-call | tf_op jit(solution)/shard_map/pallas_call | solution.py:921
  156.5 0.3 convert_reduce_fusion
  156.8 0.7 reshape.240.b_out
  157.5 0.7 reshape.241.g_one
  158.1 0.7 reshape.242.s_one
  158.8 0.7 reshape.244.b_down
  159.5 0.7 reshape.245.g_two
  160.2 0.7 reshape.246.s_two
  160.9 0.7 reshape.243.b_up
  161.6 9.2 %copy.35 = bf16[32,2,24,1536]{3,1,2,0:T(2,128)(2,1)} copy(bf16[32,2,24,1536]{3,2,1,0:T(8,128)(2,1)} %bitcast.58) | data formatting | bytes 9437184 | tf_op jit(solution)/shard_map/reshape | solution.py:699
  170.8 5.8 %copy.38 = bf16[96,8,2,1536]{3,1,2,0:T(8,128)(2,1)} copy(bf16[96,8,2,1536]{3,2,1,0:T(2,128)(2,1)} %bitcast.48) | data formatting | bytes 9437184
  176.6 0.9 copy.34
  177.5 1.2 copy.37
  178.7 96.1 %shard_map.264 = (bf16[1536,768]{1,0:T(8,128)(2,1)}, f32[1536,768]{1,0:T(8,128)}, bf16[1536,768]{1,0:T(8,128)(2,1)}, f32[768,768]{1,0:T(8,128)}, f32[768,3072]{1...) custom-call(bf16[1536,768]{1,0:T(8,128)(2,1)} %bitcast.44, ...), custom_call_target="tpu_custom_call" | custom-call | tf_op jit(solution)/shard_map/pallas_call | solution.py:944
  274.8 98.8 %shard_map.265.gm = bf16[1536,2304]{1,0:T(8,128)(2,1)} custom-call(s32[3]{0:T(128)} %lens.3, bf16[1536,768]{1,0:T(8,128)(2,1)} %get-tuple-element.56.q, bf16[1536,768]{1,0:T(8,128)(2,1)} %get-tuple-element.57.k, bf16[1536,768]{1,0:T(8,128)(2,1)} %get-tuple-element.58.v, bf16[1536,768]{1,0:T(8,128)(2,1)} %get-tuple-element.59.gj, ...), custom_call_target="tpu_custom_call" | custom-call | tf_op jit(solution)/shard_map/pallas_call | solution.py:966
  373.8 18.5 %shard_map.266 = (f32[1536,768]{1,0:T(8,128)}, f32[768,2304]{1,0:T(8,128)}, f32[1,2304]{1,0:T(1,128)}) custom-call(bf16[1536,768]{1,0:T(8,128)(2,1)} %bitcast.45, bf16[1536,2304]{1,0:T(8,128)(2,1)} %shard_map.265.gm, bf16[768,2304]{1,0:T(8,128)(2,1)} %bitcast.42, f32[1536,768]{1,0:T(8,128)} %get-tuple-element.64.g_first), custom_call_target="tpu_custom_call" | custom-call | tf_op jit(solution)/shard_map/pallas_call | solution.py:975
  392.3 0.7 slice_reduce_fusion
  393.0 0.7 slice_reduce_fusion.1
  394.0 0.6 pad.39.refs_4_
  394.7 3.4 convert.31
  398.0 0.3 fusion.1
  398.3 2.1 pad_maximum_fusion.1.refs_3_
  400.4 1.0 copy-done
  401.4 0.1 convert.30
  401.5 0.1 fusion.2
  401.7 1.2 pad_maximum_fusion.2.refs_2_
  402.8 1.1 slice-done.4
  403.9 0.4 slice-done.5
  404.3 0.7 convert.29
  405.1 0.3 fusion
  405.4 2.9 pad_maximum_fusion.refs_1_
  408.3 0.9 slice-done.1
  409.2 1.4 slice-done.2
  410.6 2.6 convert_element_type.125
  413.2 77.0 %shard_map.267 = (f32[96,768]{1,0:T(8,128)}, f32[24,3072]{1,0:T(8,128)}, f32[24,768]{1,0:T(8,128)}, f32[24,2304]{1,0:T(8,128)}, f32[16,768]{1,0:T(8,128)}) custom-call(bf16[32,96,768]{2,1,0:T(8,128)(2,1)} %bitcast.47, bf16[32,48,1536]{2,1,0:T(8,128)(2,1)} %pad_maximum_fusion.refs_1_, bf16[32,48,384]{2,1,0:T(8,128)(2,1)} %pad_maximum_fusion.2.refs_2_, ...), custom_call_target="tpu_custom_call" | custom-call | tf_op jit(solution)/shard_map/pallas_call | solution.py:832
  490.2 0.8 reshape.238
  491.0 0.6 fusion.5
  491.7 0.6 dynamic_slice.32
  492.2 0.6 dynamic_slice.27
  492.8 1.6 copy.52
  494.5 1.5 copy.53
  496.0 1.7 copy.54
  497.7 1.7 copy.55
  (54 shorter events, 0.3 us)
Async XLA Ops:
  103.6 52.9 %copy-start.2 = (bf16[32,16,128]{2,1,0:T(8,128)(2,1)S(1)}, bf16[32,16,128]{2,1,0:T(8,128)(2,1)}, u32[]{:S(2)}) copy-start(bf16[32,16,128]{2,1,0:T(8,128)(2,1)} %get-tuple-element.50) | copy-start | bytes 393220
  170.8 5.8 %copy-start.1 = (bf16[32,48,384]{2,1,0:T(8,128)(2,1)S(1)}, bf16[32,48,384]{2,1,0:T(8,128)(2,1)}, u32[]{:S(2)}) copy-start(bf16[32,48,384]{2,1,0:T(8,128)(2,1)} %get-tuple-element.52) | copy-start | bytes 3538948
  373.7 20.0 %copy-start.9 = (f32[1,768]{1,0:T(1,128)S(1)}, f32[1,768]{1,0:T(1,128)}, u32[]{:S(2)}) copy-start(f32[1,768]{1,0:T(1,128)} %get-tuple-element.71) | copy-start | bytes 9220
  373.7 20.1 %copy-start.8 = (f32[1,768]{1,0:T(1,128)S(1)}, f32[1,768]{1,0:T(1,128)}, u32[]{:S(2)}) copy-start(f32[1,768]{1,0:T(1,128)} %get-tuple-element.72) | copy-start | bytes 9220
  373.7 20.1 %copy-start.7 = (f32[1,768]{1,0:T(1,128)S(1)}, f32[1,768]{1,0:T(1,128)}, u32[]{:S(2)}) copy-start(f32[1,768]{1,0:T(1,128)} %get-tuple-element.73) | copy-start | bytes 9220
  373.7 20.2 %copy-start.3 = (f32[1,3072]{1,0:T(1,128)S(1)}, f32[1,3072]{1,0:T(1,128)}, u32[]{:S(2)}) copy-start(f32[1,3072]{1,0:T(1,128)} %get-tuple-element.74) | copy-start | bytes 36868
  373.7 20.2 %copy-start.6 = (f32[1,768]{1,0:T(1,128)S(1)}, f32[1,768]{1,0:T(1,128)}, u32[]{:S(2)}) copy-start(f32[1,768]{1,0:T(1,128)} %get-tuple-element.75) | copy-start | bytes 9220
  373.7 20.2 %copy-start.5 = (f32[1,768]{1,0:T(1,128)S(1)}, f32[1,768]{1,0:T(1,128)}, u32[]{:S(2)}) copy-start(f32[1,768]{1,0:T(1,128)} %get-tuple-element.76) | copy-start | bytes 9220
  373.7 20.2 %copy-start.4 = (f32[1,768]{1,0:T(1,128)S(1)}, f32[1,768]{1,0:T(1,128)}, u32[]{:S(2)}) copy-start(f32[1,768]{1,0:T(1,128)} %get-tuple-element.77) | copy-start | bytes 9220
  398.0 4.8 slice-start.3
  398.3 3.1 copy-start
  398.3 5.6 %slice-start.4 = ((s8[9437184]{0:T(1024)(128)(4,1)}), s8[4194304]{0:T(1024)(128)(4,1)S(1)}, s32[]{:S(2)}) async-start(s8[9437184]{0:T(1024)(128)(4,1)} %bitcast.54), calls=%async_computation.4 | async-start | bytes 8388608
  401.4 2.9 slice-start.5
  405.1 3.3 slice-start
  405.1 4.2 slice-start.1
  405.4 5.2 %slice-start.2 = ((s8[9437184]{0:T(1024)(128)(4,1)}), s8[4194304]{0:T(1024)(128)(4,1)S(1)}, s32[]{:S(2)}) async-start(s8[9437184]{0:T(1024)(128)(4,1)} %bitcast.52), calls=%async_computation.2 | async-start | bytes 8388608
